TPU v7x, 256 devices: a whole 4x4x8 slice. The times are simulated.
256 devices in a mesh: gx: 8 (over z), gy: 8 (over x, core), gz: 4 (over y).
Axes of the slice: x: 4, y: 4, z: 8, core: 2. Of those that a mesh axis runs over, the one named last changes fastest.
Arguments:
- rhs_interior: float32 [64, 8192, 512], P('gx', 'gy', 'gz'), may hold values from -9 to 9
- rhs_sep: float32 [8, 8192, 512], P('gx', 'gy', 'gz'), may hold values from -9 to 9
- lower_inv: float32 [64, 8, 4, 128, 128], P('gx', 'gy', 'gz'), may hold values from -1 to 1
- lower_off: float32 [56, 8, 4, 128, 128], P('gx', 'gy', 'gz'), may hold values from -4 to 1
- upper_inv: float32 [64, 8, 4, 128, 128], P('gx', 'gy', 'gz'), may hold values from -1 to 2
- upper_off: float32 [56, 8, 4, 128, 128], P('gx', 'gy', 'gz'), may hold values from -1 to 1
- link_into: float32 [16, 8192, 512], P('gx', 'gy', 'gz'), may hold values from 0.5 to 1.5
- link_from: float32 [16, 8192, 512], P('gx', 'gy', 'gz'), may hold values from 0.5 to 1.5
- sep_diag: float32 [8, 8192, 512], P('gx', 'gy', 'gz'), may hold values from 6 to 9
- coupling: int32 [4, 56, 8192], P('gz', 'gx', 'gy'), may hold values 0 or 1
Outputs:
- interior_solution: float32 [64, 8192, 512], P('gx', 'gy', 'gz')
- sep_solution: float32 [8, 8192, 512], P('gx', 'gy', 'gz')
All inputs are finite; a program needn't handle non-finite values. No bound on the sum of `coupling` on one device may be relied on, other than what follows from the above.
Results may differ from a plain program's by a relative error of at most 0.0001.
Values sent between devices are 32-bit elements; how exact they have to be, the bound alone decides.
No kernel may reach another device: no remote copies, remote signals or barrier semaphores. Data moves between devices by JAX's collectives and lax.ppermute only.
A program may use at most 128 MiB of HBM per device.

v0:
```python
import functools

import jax
import jax.numpy as jnp
from jax import lax
from jax.experimental import pallas as pl
from jax.experimental.pallas import tpu as pltpu
from jax.sharding import PartitionSpec as P

EPSILON = 1e-06
CONVECTION = 0.5
SHIFT = 7.5
SCALE_ONE = 2.0**-15
SCALE_TWO = 2.0**-30
AXES = ("gx", "gy", "gz")
LIMIT = 40 * 1024 * 1024

F32 = jnp.float32
BF16 = jnp.bfloat16


def halves(value):
    high = value.astype(BF16)
    low = (value - high.astype(F32)).astype(BF16)
    return high, low


def product(left, right):
    width = right[0].shape[1]
    wide = jnp.dot(left[0], jnp.concatenate(right, axis=1), preferred_element_type=F32)
    rest = jnp.dot(left[1], right[0], preferred_element_type=F32)
    return wide[:, :width] + (wide[:, width:] + rest)


def side(first, second):
    return tuple(jnp.concatenate([a, b], axis=1) for a, b in zip(first, second))


def over(first, second):
    return tuple(jnp.concatenate([a, b], axis=0) for a, b in zip(first, second))


def small(left, right):
    return product(halves(left), halves(right))


def masked(value, gate):
    return tuple(part * gate for part in value)


def column(gates, index, like):
    return jnp.broadcast_to(gates[:, index : index + 1], like).astype(BF16)


def forward_kernel(
    rhs_hbm, linv_hbm, loff_hbm, uinv_hbm, uoff_hbm, coupling_hbm, sep_hbm, from_hbm,
    m_ref, p_ref, t_ref, gates_ref, mats_ref,
    rhs, linv, loff, uinv, uoff, coupling, sep, link, sems,
):
    planes = rhs.shape[0]
    copies = {}

    def fetch(name, source, target):
        copies[name] = pltpu.make_async_copy(source, target, sems.at[len(copies)])
        copies[name].start()

    fetch("coupling", coupling_hbm.at[0], coupling)
    fetch("linv", linv_hbm.at[:, 0, 0], linv)
    fetch(0, rhs_hbm.at[0], rhs.at[0])
    fetch("loff", loff_hbm.at[:, 0, 0], loff)
    fetch("uinv", uinv_hbm.at[:, 0, 0], uinv)
    fetch("uoff", uoff_hbm.at[:, 0, 0], uoff)
    for plane in range(1, planes):
        fetch(plane, rhs_hbm.at[plane], rhs.at[plane])
    fetch("sep", sep_hbm.at[0], sep)
    fetch("link", from_hbm, link)

    copies["coupling"].wait()
    gate_rows = coupling[...].astype(F32)
    rows = [gate_rows[p : p + 1] for p in range(planes - 1)]
    prefix = [jnp.ones_like(rows[0])]
    for row in rows:
        prefix.append(prefix[-1] * row)
    open_any = [jnp.max(row, axis=1, keepdims=True) for row in prefix]
    gates = jnp.transpose(jnp.concatenate(rows + [jnp.zeros_like(rows[0])] + prefix, axis=0))
    gates_ref[...] = gates
    like = rhs.shape[1:]

    for name in ("linv", "loff", "uinv", "uoff"):
        copies[name].wait()
    lower = [halves(linv[p]) for p in range(planes)]
    upper = [halves(uinv[p]) for p in range(planes)]
    links_l, links_u = [None], []
    for p in range(1, planes):
        merged = product(halves(loff[p - 1]), lower[p])
        mats_ref[p - 1] = merged
        links_l.append(halves(merged))
    for p in range(planes - 1):
        merged = product(halves(uoff[p]), upper[p])
        mats_ref[planes - 1 + p] = merged
        links_u.append(halves(merged))
    back = [upper[0]]
    mats_ref[2 * planes - 2] = uinv[0]
    tail = None
    for p in range(1, planes):
        step = (-open_any[p]) * mats_ref[planes - 1 + p - 1]
        tail = step if tail is None else small(step, tail)
        full = product(upper[p], halves(tail))
        mats_ref[2 * planes - 2 + p] = full
        back.append(halves(full))

    total = None
    pending = None
    previous = None
    for p in range(planes):
        copies[p].wait()
        source = halves(rhs[p])
        if p == 0:
            running = product(source, lower[0])
        else:
            gated = masked(previous, -column(gates, p - 1, like))
            running = product(side(source, gated), over(lower[p], links_l[p]))
        t_ref[p] = running
        previous = halves(running)
        part = previous if p == 0 else masked(previous, column(gates, planes + p, like))
        if p % 2 == 0:
            pending = part
        else:
            term = product(side(pending, part), over(back[p - 1], back[p]))
            total = term if total is None else total + term
    copies["link"].wait()
    m_ref[...] = link[1] * product(previous, upper[planes - 1])
    copies["sep"].wait()
    p_ref[...] = sep[...] + link[0] * total


def backward_kernel(t_ref, gates_ref, mats_ref, linv_ref, uinv_ref, x_ref, apply_ref, sweep_ref):
    planes = t_ref.shape[0]
    gates = gates_ref[...]
    like = t_ref.shape[1:]
    upper = [halves(uinv_ref[p, 0, 0]) for p in range(planes)]
    links_u = [halves(mats_ref[planes - 1 + p]) for p in range(planes - 1)]
    size = like[1]

    def keep(ref, index, value):
        for part in range(2):
            ref[part, index * size : (index + 1) * size, :] = value[part]

    open_any = [jnp.max(gates[:, planes + p : planes + p + 1], axis=0, keepdims=True) for p in range(planes)]
    first = halves(linv_ref[0, 0, 0])
    last = halves(linv_ref[planes - 1, 0, 0])
    running = linv_ref[0, 0, 0]
    for p in range(planes):
        if p > 0:
            running = product(halves(running), halves((-open_any[p]) * mats_ref[p - 1]))
        now = halves(running) if p > 0 else first
        full = halves(mats_ref[2 * planes - 2 + p])
        keep(apply_ref, p, halves(product(now, full)))
        if p < planes - 1:
            keep(sweep_ref, 2 * p, halves(product(now, upper[p])))
            keep(sweep_ref, 2 * p + 1, links_u[p])
        else:
            keep(apply_ref, planes, halves(product(last, full)))
            keep(apply_ref, planes + 1, halves(product(last, upper[p])))
            keep(apply_ref, planes + 2, halves(product(now, upper[p])))

    solved = product(halves(t_ref[planes - 1]), upper[planes - 1])
    x_ref[planes - 1] = solved
    for p in range(planes - 2, -1, -1):
        gated = masked(halves(solved), -column(gates, p, like))
        solved = product(side(halves(t_ref[p]), gated), over(upper[p], links_u[p]))
        x_ref[p] = solved


def block(ref, first, count, size=128):
    return ref[0, first * size : (first + count) * size, :], ref[1, first * size : (first + count) * size, :]


def slab(vector, following, into_ref, gates, apply_ref):
    planes = 8
    like = vector.shape
    near = halves(into_ref[0] * vector)
    far = halves(into_ref[1] * following)
    cuts = [None] + [column(gates, planes + p, like) for p in range(1, planes)]
    gated = [near] + [masked(near, cuts[p]) for p in range(1, planes)]
    far_end = product(side(far, gated[-1]), block(apply_ref, planes + 1, 2))
    near_end = product(masked(far, cuts[-1]), block(apply_ref, planes, 1))
    for p in range(0, planes, 2):
        near_end = near_end + product(side(gated[p], gated[p + 1]), block(apply_ref, p, 2))
    return near_end, far_end


def inner_stencil(vector, diagonal):
    zero_row = jnp.zeros_like(vector[:1])
    zero_column = jnp.zeros_like(vector[:, :1])
    up = jnp.concatenate([zero_row, vector[:-1]], axis=0)
    down = jnp.concatenate([vector[1:], zero_row], axis=0)
    left = jnp.concatenate([zero_column, vector[:, :-1]], axis=1)
    right = jnp.concatenate([vector[:, 1:], zero_column], axis=1)
    return (
        (diagonal - SHIFT) * vector
        - (up + down)
        - (1.0 + CONVECTION) * left
        - (1.0 - CONVECTION) * right
    )


def put_rims(fields, rims):
    row_first, row_last, column_first, column_last = rims
    for index, field in enumerate(fields):
        row_first[index : index + 1, :] = field[:1]
        row_last[index : index + 1, :] = field[-1:]
        turned = jnp.transpose(field)
        column_first[index : index + 1, :] = turned[:1]
        column_last[index : index + 1, :] = turned[-1:]


def rim_columns(column_low, column_high):
    stacked = jnp.concatenate([column_low[...], column_high[...]] * 2, axis=0)
    return jnp.transpose(stacked)


def rim_terms(index, rows, turned, row_low, row_high, width):
    start, stop, total = rows
    count = stop - start
    lane = lax.broadcasted_iota(jnp.int32, (count, width), 1)
    line = lax.broadcasted_iota(jnp.int32, (count, width), 0)
    low = (1.0 + CONVECTION) * turned[start:stop, index : index + 1]
    high = (1.0 - CONVECTION) * turned[start:stop, index + 2 : index + 3]
    value = jnp.where(lane == 0, low, jnp.where(lane == width - 1, high, 0.0))
    if start == 0:
        value = value + jnp.where(line == 0, row_low[index : index + 1, :], 0.0)
    if stop == total:
        value = value + jnp.where(line == count - 1, row_high[index : index + 1, :], 0.0)
    return value


def first_kernel(
    flags, p_ref, m_ref, m_prev, p_next, into_ref, from_ref, diag_ref, gates_ref, apply_ref,
    k_ref, kn_ref, mm_ref, loc_ref, row_first, row_last, column_first, column_last,
):
    vector = p_ref[...] + m_prev[...]
    following = (p_next[...] + m_ref[...]) * flags[1]
    k_ref[...] = vector
    kn_ref[...] = following
    put_rims((vector, following), (row_first, row_last, column_first, column_last))
    near, far = slab(vector, following, into_ref, gates_ref[...], apply_ref)
    mm_ref[...] = from_ref[1] * far
    loc_ref[...] = inner_stencil(vector, diag_ref[0]) - from_ref[0] * near


def second_kernel(
    flags, loc_ref, mm_ref, mm_prev, loc_next, row_low, row_high, column_low, column_high,
    into_ref, from_ref, diag_ref, gates_ref, apply_ref,
    k_ref, kn_ref, mma_ref, mmb_ref, loca_ref, locb_ref, row_first, row_last, column_first, column_last,
):
    count, width = loc_ref.shape
    half = count // 2
    turned = rim_columns(column_low, column_high)
    rows = (0, count, count)
    vector = loc_ref[...] - mm_prev[...] - rim_terms(0, rows, turned, row_low, row_high, width)
    following = loc_next[...] - mm_ref[...] - rim_terms(1, rows, turned, row_low, row_high, width)
    following = following * flags[1]
    k_ref[...] = vector
    kn_ref[...] = following
    put_rims((vector, following), (row_first, row_last, column_first, column_last))
    near, far = slab(vector, following, into_ref, gates_ref[...], apply_ref)
    sent = from_ref[1] * far
    mma_ref[...] = sent[:half]
    mmb_ref[...] = sent[half:]
    local = inner_stencil(vector, diag_ref[0]) - from_ref[0] * near
    loca_ref[...] = local[:half]
    locb_ref[...] = local[half:]


def sums_kernel(
    flags, k0, k0n, k1, k1n, mma, mmb_prev, loca, locb, loca_next, row_low, row_high, column_low, column_high,
    out_ref,
):
    count, width = k0.shape
    half = count // 2
    turned = rim_columns(column_low, column_high)
    top, bottom = (0, half, count), (half, count, count)
    own_low = loca[...] - rim_terms(0, top, turned, row_low, row_high, width)
    own_high = locb[...] - mmb_prev[...] - rim_terms(0, bottom, turned, row_low, row_high, width)
    next_low = loca_next[...] - mma[...] - rim_terms(1, top, turned, row_low, row_high, width)
    groups = (
        (k0[half:], k1[half:] * SCALE_ONE, own_high * SCALE_TWO, None),
        (k0n[:half], k1n[:half] * SCALE_ONE, next_low * SCALE_TWO, flags[1]),
        (k0[:half], k1[:half] * SCALE_ONE, own_low * SCALE_TWO, flags[0]),
    )
    totals = [0.0] * 6
    for zero, one, two, weight in groups:
        pairs = ((zero, zero), (zero, one), (one, one), (zero, two), (one, two), (two, two))
        for index, (left, right) in enumerate(pairs):
            value = jnp.sum((left * right).reshape(half // 8, 8, width), axis=0)
            totals[index] = totals[index] + (value if weight is None else value * weight)
    lane = lax.broadcasted_iota(jnp.int32, (1, width), 1)
    line = jnp.zeros((1, width), F32)
    for index in range(6):
        line = jnp.where(lane == index, jnp.sum(totals[index]), line)
    out_ref[...] = line


def weights(sums):
    g00, g01, g11, g02, g12, g22 = sums
    one, two = 1.0 / SCALE_ONE, 1.0 / SCALE_TWO
    ratio = SCALE_ONE / SCALE_TWO
    square = g00 + EPSILON
    beta = jnp.sqrt(square)
    g00, g01s, g11s = g00 / square, g01 / square, g11 / square
    g02s, g12s, g22s = g02 / square, g12 / square, g22 / square
    lag = EPSILON / square
    delta = g01s * one - SHIFT * lag
    h11 = delta + SHIFT
    small_delta = delta * SCALE_ONE
    qq = (g11s - 2.0 * small_delta * g01s + small_delta * small_delta * g00) * one * one
    qq = jnp.maximum(qq, 0.0)
    h21 = jnp.sqrt(qq + EPSILON)
    inverse = 1.0 / h21
    gap = delta / ratio
    ku = (g02s - gap * g01s) * (two * inverse)
    kq = h11 * lag * inverse
    h12 = ku + SHIFT * kq
    qu = (g12s - gap * g11s - small_delta * g02s + small_delta * gap * g01s) * one * inverse * (two * inverse)
    vv = qq * inverse * inverse
    h22 = qu + SHIFT * vv
    turn = h22 - SHIFT
    uu = (g22s - 2.0 * gap * g12s + gap * gap * g11s) * (two * inverse) * (two * inverse)
    rr = uu + turn * turn * vv + h12 * h12 * g00 - 2.0 * turn * qu - 2.0 * h12 * ku + 2.0 * turn * h12 * kq
    h32 = jnp.sqrt(jnp.maximum(rr, 0.0) + EPSILON)
    radius = jnp.sqrt(h11 * h11 + h21 * h21)
    cosine = h11 / radius
    sine = h21 / radius
    upper_entry = cosine * h12 + sine * h22
    lower_entry = cosine * h22 - sine * h12
    second = jnp.sqrt(lower_entry * lower_entry + h32 * h32)
    weight_two = -beta * sine * lower_entry / (second * second)
    weight_one = (beta * cosine - upper_entry * weight_two) / radius
    scaled_two = weight_two * inverse / beta
    return weight_one / beta - scaled_two * delta, scaled_two


def final_kernel(
    gathered, k0, k0n, k1, k1n, into_ref, gates_ref, apply_ref, sweep_ref, x_ref,
    out_hbm, sep_hbm, out, sep, sems,
):
    planes = x_ref.shape[0]
    line = jnp.sum(gathered[...], axis=0, keepdims=True)
    lane = lax.broadcasted_iota(jnp.int32, line.shape, 1)
    sums = [jnp.sum(jnp.where(lane == index, line, 0.0), axis=1, keepdims=True) for index in range(6)]
    one, two = weights(sums)
    vector = one * k0[...] + two * k1[...]
    following = one * k0n[...] + two * k1n[...]
    sep[...] = vector
    copies = [pltpu.make_async_copy(sep, sep_hbm.at[0], sems.at[planes])]
    copies[0].start()
    gates = gates_ref[...]
    like = vector.shape
    near = halves(into_ref[0] * vector)
    far = halves(into_ref[1] * following)
    running = None
    for p in range(planes - 1, -1, -1):
        gated = near if p == 0 else masked(near, column(gates, planes + p, like))
        if running is None:
            running = product(side(far, gated), block(apply_ref, planes + 1, 2))
        else:
            other = masked(halves(running), -column(gates, p, like))
            running = product(side(gated, other), block(sweep_ref, 2 * p, 2))
        out[p] = x_ref[p] + running
        copies.append(pltpu.make_async_copy(out.at[p], out_hbm.at[p], sems.at[p]))
        copies[-1].start()
    for copy in copies:
        copy.wait()


def inside(count):
    return [pl.BlockSpec(memory_space=pltpu.VMEM)] * count


def outside(count):
    return [pl.BlockSpec(memory_space=pl.ANY)] * count


SCALARS = [pl.BlockSpec(memory_space=pltpu.SMEM)]


def shape(*sizes, dtype=F32):
    return jax.ShapeDtypeStruct(sizes, dtype)


def call(kernel, name, in_specs, out_shape, out_specs, scratch=(), flops=0, moved=0):
    return pl.pallas_call(
        kernel,
        name=name,
        in_specs=in_specs,
        out_shape=out_shape,
        out_specs=out_specs,
        scratch_shapes=list(scratch),
        compiler_params=pltpu.CompilerParams(vmem_limit_bytes=LIMIT),
        cost_estimate=pl.CostEstimate(flops=flops, bytes_accessed=moved, transcendentals=0),
    )


def body(
    rhs_interior, rhs_sep, lower_inv, lower_off, upper_inv, upper_off, link_into, link_from, sep_diag, coupling
):
    planes, count, width = rhs_interior.shape
    half = count // 2
    slabs, blocks, lines = (lax.axis_size(axis) for axis in AXES)
    place = lax.axis_index("gx")
    flags = jnp.stack([place == 0, place < slabs - 1]).astype(F32)
    plane = shape(count, width)
    dense = 2 * 2 * count * width * width

    def along(value, axis, by):
        size = lax.axis_size(axis)
        pairs = [(i, i + by) for i in range(size) if 0 <= i + by < size]
        return lax.ppermute(value, axis, pairs)

    def rims(row_first, row_last, column_first, column_last):
        return (
            along(row_last, "gy", 1),
            along(row_first, "gy", -1),
            along(column_last, "gz", 1),
            along(column_first, "gz", -1),
        )

    rim_shapes = [shape(2, width), shape(2, width), shape(2, count), shape(2, count)]

    m, p, t, gates, mats = call(
        forward_kernel,
        "forward",
        outside(8),
        [plane, plane, shape(planes, count, width), shape(count, 2 * planes), shape(3 * planes - 2, width, width)],
        inside(5),
        [
            pltpu.VMEM((planes, count, width), F32),
            pltpu.VMEM((planes, width, width), F32),
            pltpu.VMEM((planes - 1, width, width), F32),
            pltpu.VMEM((planes, width, width), F32),
            pltpu.VMEM((planes - 1, width, width), F32),
            pltpu.VMEM((planes - 1, count), jnp.int32),
            pltpu.VMEM((count, width), F32),
            pltpu.VMEM((2, count, width), F32),
            pltpu.SemaphoreType.DMA((planes + 7,)),
        ],
        flops=dense * 24,
        moved=12 << 20,
    )(rhs_interior, lower_inv, lower_off, upper_inv, upper_off, coupling, rhs_sep, link_from)
    m_prev = along(m, "gx", 1)
    p_next = along(p, "gx", -1)
    x, applied, swept = call(
        backward_kernel,
        "backward",
        inside(5),
        [
            shape(planes, count, width),
            shape(2, (planes + 3) * width, width, dtype=BF16),
            shape(2, (2 * planes - 2) * width, width, dtype=BF16),
        ],
        inside(3),
        flops=dense * 20,
        moved=12 << 20,
    )(t, gates, mats, lower_inv, upper_inv)
    k0, k0n, mm, loc, *edges = call(
        first_kernel,
        "first",
        SCALARS + inside(9),
        [plane] * 4 + rim_shapes,
        inside(8),
        flops=dense * 11,
        moved=4 << 20,
    )(flags, p, m, m_prev, p_next, link_into, link_from, sep_diag, gates, applied)
    mm_prev = along(mm, "gx", 1)
    loc_next = along(loc, "gx", -1)
    arrived = rims(*edges)
    part = shape(half, width)
    k1, k1n, mma, mmb, loca, locb, *edges = call(
        second_kernel,
        "second",
        SCALARS + inside(13),
        [plane] * 2 + [part] * 4 + rim_shapes,
        inside(10),
        flops=dense * 11,
        moved=4 << 20,
    )(flags, loc, mm, mm_prev, loc_next, *arrived, link_into, link_from, sep_diag, gates, applied)
    mmb_prev = along(mmb, "gx", 1)
    loca_next = along(loca, "gx", -1)
    arrived = rims(*edges)
    line = call(
        sums_kernel,
        "sums",
        SCALARS + inside(13),
        shape(1, width),
        pl.BlockSpec(memory_space=pltpu.VMEM),
        flops=dense,
        moved=4 << 20,
    )(flags, k0, k0n, k1, k1n, mma, mmb_prev, loca, locb, loca_next, *arrived)
    copies = jnp.broadcast_to(line, (slabs * blocks * lines, width))
    gathered = lax.all_to_all(copies, AXES, 0, 0, tiled=True)
    interior, separator = call(
        final_kernel,
        "final",
        inside(10),
        [shape(planes, count, width), shape(1, count, width)],
        outside(2),
        [
            pltpu.VMEM((planes, count, width), F32),
            pltpu.VMEM((count, width), F32),
            pltpu.SemaphoreType.DMA((planes + 1,)),
        ],
        flops=dense * 16,
        moved=12 << 20,
    )(gathered, k0, k0n, k1, k1n, link_into, gates, applied, swept, x)
    return interior, separator


def solution(mesh):
    field = P(*AXES)
    factor = P(*AXES, None, None)
    return jax.shard_map(
        body,
        mesh=mesh,
        in_specs=(field, field, factor, factor, factor, factor, field, field, field, P("gz", "gx", "gy")),
        out_specs=(field, field),
        check_vma=False,
    )
```

profile of v0, /device:TPU:1, one launch (start us, length us, event | category | flops | bytes accessed | tf_op | source)
XLA Modules:
  0.0 122.3 jit_solution(181598837047351776)
XLA Ops:
  0.6 0.8 copy.13.coupling_hbm
  1.4 0.0 copy-start.1
  1.4 1.2 copy-done.1
  2.6 0.0 copy-start.6
  2.6 1.0 copy-done.6
  3.7 1.0 copy-done.8
  4.7 0.0 copy-start.12
  4.7 1.0 copy-done.12
  5.7 0.0 copy-start.13
  5.7 1.0 copy-done.13
  6.8 0.0 copy-start.14
  6.8 1.0 copy-done.14
  7.8 0.0 copy-start.5
  7.8 9.2 %forward.1 = (f32[1024,128]{1,0:T(8,128)}, f32[1024,128]{1,0:T(8,128)}, f32[8,1024,128]{2,1,0:T(8,128)S(1)}, f32[1024,16]{1,0:T(8,128)S(1)}, f32[22,128,128]{2,1,0:T(8,128)S(1)}) custom-call(f32[8,1024,128]{2,1,0:T(8,128)} %rhs_hbm.1, f32[8,1,1,128,128]{4,3,2,1,0:T(8,128)S(1)} %copy-done.6, f32[7,1,1,128,128]{4,3,2,1,0:T(8,128)S(1)} %copy-done.13, ...), custom_call_target="tpu_custom_call" | custom-call | flops 1610612736 | bytes 12582912 | tf_op jit(solution)/shard_map/forward/pallas_call | solution.py:431
  17.0 0.0 copy-start.3
  17.0 2.0 %copy-done.3 = f32[8,1024,128]{2,1,0:T(8,128)} copy-done((f32[8,1024,128]{2,1,0:T(8,128)}, f32[8,1024,128]{2,1,0:T(8,128)S(1)}, u32[]{:S(2)}) %copy-start.3) | copy-done | bytes 4194328
  19.0 0.0 copy-start.10
  19.0 1.1 copy-done.10
  20.1 0.0 copy-start
  20.1 0.0 copy-start.2
  20.1 1.4 %collective-permute-start.1 = (f32[1024,128]{1,0:T(8,128)}, f32[1024,128]{1,0:T(8,128)}, u32[]{:S(2)}, u32[]{:S(2)}) collective-permute-start(f32[1024,128]{1,0:T(8,128)} %get-tuple-element.28.p_ref), channel_id=1, source_target_pairs={{32,0},{64,32},{96,64},{128,96},{160,128},{192,160},{224,192},{33,... | collective-permute-start | bytes 1572872 | tf_op jit(solution)/shard_map/ppermute | solution.py:419
  21.5 5.8 %collective-permute-start = (f32[1024,128]{1,0:T(8,128)}, f32[1024,128]{1,0:T(8,128)}, u32[]{:S(2)}, u32[]{:S(2)}) collective-permute-start(f32[1024,128]{1,0:T(8,128)} %get-tuple-element.29.m_ref), channel_id=1, source_target_pairs={{0,32},{32,64},{64,96},{96,128},{128,160},{160,192},{192,224},{1,3... | collective-permute-start | bytes 1572872 | tf_op jit(solution)/shard_map/ppermute | solution.py:419
  27.3 0.1 add_convert_fusion.flags
  27.4 0.0 copy-start.4
  27.4 2.2 %copy-done.4 = f32[8,1024,128]{2,1,0:T(8,128)S(1)} copy-done((f32[8,1024,128]{2,1,0:T(8,128)S(1)}, f32[8,1024,128]{2,1,0:T(8,128)}, u32[]{:S(2)}) %copy-start.4) | copy-done | bytes 4194328
  29.6 1.0 copy-done.7
  30.6 1.0 copy-done.9
  31.7 1.4 %copy-done.11 = f32[22,128,128]{2,1,0:T(8,128)S(1)} copy-done((f32[22,128,128]{2,1,0:T(8,128)S(1)}, f32[22,128,128]{2,1,0:T(8,128)}, u32[]{:S(2)}) %copy-start.11) | copy-done | bytes 1441816
  33.1 3.9 %backward.1 = (f32[8,1024,128]{2,1,0:T(8,128)S(1)}, bf16[2,1408,128]{2,1,0:T(8,128)(2,1)S(1)}, bf16[2,1792,128]{2,1,0:T(8,128)(2,1)S(1)}) custom-call(f32[8,1024,128]{2,1,0:T(8,128)S(1)} %copy-done.4, f32[1024,16]{1,0:T(8,128)S(1)} %get-tuple-element.30.gates_ref, f32[22,128,128]{2,1,0:T(8,128)S(1)} %copy-done.11, f32[8,1,1,128,128]{4,3,2,1,0:T(8,128)S(1)} %copy-done.7, ...), custom_call_target="tpu_custom_call" | custom-call | flops 1342177280 | bytes 12582912 | tf_op jit(solution)/shard_map/backward/pallas_call | solution.py:453
  36.9 0.0 collective-permute-done.1.p_next
  36.9 0.0 collective-permute-done.m_prev
  36.9 0.0 copy-done.5
  36.9 0.0 copy-done
  37.0 0.0 copy-done.2
  37.0 3.9 %first.1 = (f32[1024,128]{1,0:T(8,128)S(1)}, f32[1024,128]{1,0:T(8,128)S(1)}, f32[1024,128]{1,0:T(8,128)S(1)}, f32[1024,128]{1,0:T(8,128)S(1)}, f32[2,128]{1,0:T...) custom-call(f32[2]{0:T(128)S(1)} %add_convert_fusion.flags, ...), custom_call_target="tpu_custom_call" | custom-call | flops 738197504 | bytes 4194304 | tf_op jit(solution)/shard_map/first/pallas_call | solution.py:466
  40.8 1.3 %collective-permute-start.3 = (f32[1024,128]{1,0:T(8,128)S(1)}, f32[1024,128]{1,0:T(8,128)S(1)}, u32[]{:S(2)}, u32[]{:S(2)}) collective-permute-start(f32[1024,128]{1,0:T(8,128)S(1)} %get-tuple-element.36.loc_ref), channel_id=1, source_target_pairs={{32,0},{64,32},{96,64},{128,96},{160,128},{192,160},{224,192},{33,... | collective-permute-start | bytes 1572872 | tf_op jit(solution)/shard_map/ppermute | solution.py:419
  42.1 4.6 %collective-permute-start.2 = (f32[1024,128]{1,0:T(8,128)S(1)}, f32[1024,128]{1,0:T(8,128)S(1)}, u32[]{:S(2)}, u32[]{:S(2)}) collective-permute-start(f32[1024,128]{1,0:T(8,128)S(1)} %get-tuple-element.37.mm_ref), channel_id=1, source_target_pairs={{0,32},{32,64},{64,96},{96,128},{128,160},{160,192},{192,224},{1,3... | collective-permute-start | bytes 1572872 | tf_op jit(solution)/shard_map/ppermute | solution.py:419
  46.7 3.7 %collective-permute-start.6 = (f32[2,1024]{1,0:T(2,128)S(1)}, f32[2,1024]{1,0:T(2,128)S(1)}, u32[]{:S(2)}, u32[]{:S(2)}) collective-permute-start(f32[2,1024]{1,0:T(2,128)S(1)} %get-tuple-element.40), channel_id=1, source_target_pairs={{0,1},{1,2},{2,3},{4,5},{5,6},{6,7},{8,9},{9,10},{10,11},{12,13},{... | collective-permute-start | bytes 24584 | tf_op jit(solution)/shard_map/ppermute | solution.py:419
  50.5 1.3 %collective-permute-start.7 = (f32[2,1024]{1,0:T(2,128)S(1)}, f32[2,1024]{1,0:T(2,128)S(1)}, u32[]{:S(2)}, u32[]{:S(2)}) collective-permute-start(f32[2,1024]{1,0:T(2,128)S(1)} %get-tuple-element.41), channel_id=1, source_target_pairs={{1,0},{2,1},{3,2},{5,4},{6,5},{7,6},{9,8},{10,9},{11,10},{13,12},{... | collective-permute-start | bytes 24584 | tf_op jit(solution)/shard_map/ppermute | solution.py:419
  51.8 5.2 %collective-permute-start.4 = (f32[2,128]{1,0:T(2,128)S(1)}, f32[2,128]{1,0:T(2,128)S(1)}, u32[]{:S(2)}, u32[]{:S(2)}) collective-permute-start(f32[2,128]{1,0:T(2,128)S(1)} %get-tuple-element.38), channel_id=1, source_target_pairs={{0,4},{4,8},{8,12},{12,16},{16,20},{20,24},{24,28},{1,5},{5,9},{9,... | collective-permute-start | bytes 3080 | tf_op jit(solution)/shard_map/ppermute | solution.py:419
  57.0 0.7 collective-permute-done.4.row_low
  57.7 1.9 %collective-permute-start.5 = (f32[2,128]{1,0:T(2,128)S(1)}, f32[2,128]{1,0:T(2,128)S(1)}, u32[]{:S(2)}, u32[]{:S(2)}) collective-permute-start(f32[2,128]{1,0:T(2,128)S(1)} %get-tuple-element.39), channel_id=1, source_target_pairs={{4,0},{8,4},{12,8},{16,12},{20,16},{24,20},{28,24},{5,1},{9,5},{13... | collective-permute-start | bytes 3080 | tf_op jit(solution)/shard_map/ppermute | solution.py:419
  59.6 3.5 %collective-permute-done.5.row_high = f32[2,128]{1,0:T(2,128)S(1)} collective-permute-done((f32[2,128]{1,0:T(2,128)S(1)}, f32[2,128]{1,0:T(2,128)S(1)}, u32[]{:S(2)}, u32[]{:S(2)}) %collective-permute-start.5) | collective-permute-done | bytes 1056 | tf_op jit(solution)/shard_map/ppermute | solution.py:419
  63.1 0.0 collective-permute-done.6.column_low
  63.1 0.0 collective-permute-done.7.column_high
  63.1 0.0 collective-permute-done.3.loc_next
  63.1 0.0 collective-permute-done.2.mm_prev
  63.1 3.8 %second.1 = (f32[1024,128]{1,0:T(8,128)S(1)}, f32[1024,128]{1,0:T(8,128)S(1)}, f32[512,128]{1,0:T(8,128)S(1)}, f32[512,128]{1,0:T(8,128)S(1)}, f32[512,128]{1,0:...) custom-call(f32[2]{0:T(128)S(1)} %add_convert_fusion.flags, ...), custom_call_target="tpu_custom_call" | custom-call | flops 738197504 | bytes 4194304 | tf_op jit(solution)/shard_map/second/pallas_call | solution.py:479
  66.9 3.6 %collective-permute-start.8 = (f32[512,128]{1,0:T(8,128)S(1)}, f32[512,128]{1,0:T(8,128)S(1)}, u32[]{:S(2)}, u32[]{:S(2)}) collective-permute-start(f32[512,128]{1,0:T(8,128)S(1)} %get-tuple-element.45), channel_id=1, source_target_pairs={{0,32},{32,64},{64,96},{96,128},{128,160},{160,192},{192,224},{1,3... | collective-permute-start | bytes 786440 | tf_op jit(solution)/shard_map/ppermute | solution.py:419
  70.6 1.3 %collective-permute-start.9 = (f32[512,128]{1,0:T(8,128)S(1)}, f32[512,128]{1,0:T(8,128)S(1)}, u32[]{:S(2)}, u32[]{:S(2)}) collective-permute-start(f32[512,128]{1,0:T(8,128)S(1)} %get-tuple-element.46.loca), channel_id=1, source_target_pairs={{32,0},{64,32},{96,64},{128,96},{160,128},{192,160},{224,192},{33,... | collective-permute-start | bytes 786440 | tf_op jit(solution)/shard_map/ppermute | solution.py:419
  71.9 4.3 %collective-permute-start.12 = (f32[2,1024]{1,0:T(2,128)S(1)}, f32[2,1024]{1,0:T(2,128)S(1)}, u32[]{:S(2)}, u32[]{:S(2)}) collective-permute-start(f32[2,1024]{1,0:T(2,128)S(1)} %get-tuple-element.50), channel_id=1, source_target_pairs={{0,1},{1,2},{2,3},{4,5},{5,6},{6,7},{8,9},{9,10},{10,11},{12,13},{... | collective-permute-start | bytes 24584 | tf_op jit(solution)/shard_map/ppermute | solution.py:419
  76.2 1.3 %collective-permute-start.13 = (f32[2,1024]{1,0:T(2,128)S(1)}, f32[2,1024]{1,0:T(2,128)S(1)}, u32[]{:S(2)}, u32[]{:S(2)}) collective-permute-start(f32[2,1024]{1,0:T(2,128)S(1)} %get-tuple-element.51), channel_id=1, source_target_pairs={{1,0},{2,1},{3,2},{5,4},{6,5},{7,6},{9,8},{10,9},{11,10},{13,12},{... | collective-permute-start | bytes 24584 | tf_op jit(solution)/shard_map/ppermute | solution.py:419
  77.5 2.5 %collective-permute-start.10 = (f32[2,128]{1,0:T(2,128)S(1)}, f32[2,128]{1,0:T(2,128)S(1)}, u32[]{:S(2)}, u32[]{:S(2)}) collective-permute-start(f32[2,128]{1,0:T(2,128)S(1)} %get-tuple-element.48), channel_id=1, source_target_pairs={{0,4},{4,8},{8,12},{12,16},{16,20},{20,24},{24,28},{1,5},{5,9},{9,... | collective-permute-start | bytes 3080 | tf_op jit(solution)/shard_map/ppermute | solution.py:419
  80.0 0.7 collective-permute-done.10.row_low
  80.7 1.9 %collective-permute-start.11 = (f32[2,128]{1,0:T(2,128)S(1)}, f32[2,128]{1,0:T(2,128)S(1)}, u32[]{:S(2)}, u32[]{:S(2)}) collective-permute-start(f32[2,128]{1,0:T(2,128)S(1)} %get-tuple-element.49), channel_id=1, source_target_pairs={{4,0},{8,4},{12,8},{16,12},{20,16},{24,20},{28,24},{5,1},{9,5},{13... | collective-permute-start | bytes 3080 | tf_op jit(solution)/shard_map/ppermute | solution.py:419
  82.6 3.5 %collective-permute-done.11.row_high = f32[2,128]{1,0:T(2,128)S(1)} collective-permute-done((f32[2,128]{1,0:T(2,128)S(1)}, f32[2,128]{1,0:T(2,128)S(1)}, u32[]{:S(2)}, u32[]{:S(2)}) %collective-permute-start.11) | collective-permute-done | bytes 1056 | tf_op jit(solution)/shard_map/ppermute | solution.py:419
  86.1 0.0 collective-permute-done.12.column_low
  86.1 0.0 collective-permute-done.13.column_high
  86.1 0.0 collective-permute-done.8.mmb_prev
  86.1 0.0 collective-permute-done.9.loca_next
  86.1 1.6 %sums.1 = f32[1,128]{1,0:T(1,128)S(1)} custom-call(f32[2]{0:T(128)S(1)} %add_convert_fusion.flags, f32[1024,128]{1,0:T(8,128)S(1)} %get-tuple-element.34.k0, f32[1024,128]{1,0:T(8,128)S(1)} %get-tuple-element.35.k0n, f32[1024,128]{1,0:T(8,128)S(1)} %get-tuple-element.42.k1, f32[1024,128]{1,0:T(8,128)S(1)} %get-tuple-element.43.k1n, ...), custom_call_target="tpu_custom_call" | custom-call | flops 67108864 | bytes 4194304 | tf_op jit(solution)/shard_map/sums/pallas_call | solution.py:491
  87.7 0.1 broadcast_in_dim.2
  87.8 30.7 %all_to_all.8 = f32[256,1,128]{2,1,0:T(1,128)S(1)} all-to-all(f32[256,1,128]{2,1,0:T(1,128)S(1)} %broadcast_in_dim.2), channel_id=1, replica_groups=mesh['gx'=8,'gy'=8,'gz'=4] {'gx','gy','gz'}, dimensions={0} | all-to-all | bytes 262144 | tf_op jit(solution)/shard_map/all_to_all | solution.py:501
  118.5 3.6 %final.1 = (f32[8,1024,128]{2,1,0:T(8,128)}, f32[1,1024,128]{2,1,0:T(8,128)}) custom-call(f32[256,128]{1,0:T(8,128)S(1)} %bitcast.4, f32[1024,128]{1,0:T(8,128)S(1)} %get-tuple-element.34.k0, f32[1024,128]{1,0:T(8,128)S(1)} %get-tuple-element.35.k0n, f32[1024,128]{1,0:T(8,128)S(1)} %get-tuple-element.42.k1, f32[1024,128]{1,0:T(8,128)S(1)} %get-tuple-element.43.k1n, ...), custom_call_target="tpu_custom_call" | custom-call | flops 1073741824 | bytes 12582912 | tf_op jit(solution)/shard_map/final/pallas_call | solution.py:502
  (4 shorter events, 0.0 us)
Async XLA Ops:
  1.4 1.2 %copy-start.1 = (f32[2,1024,128]{2,1,0:T(8,128)S(1)}, f32[2,1024,128]{2,1,0:T(8,128)}, u32[]{:S(2)}) copy-start(f32[2,1024,128]{2,1,0:T(8,128)} %from_ref.3) | copy-start | bytes 3145732
  2.6 1.0 copy-start.6
  3.7 1.0 copy-start.8
  4.7 1.0 copy-start.12
  5.7 1.0 copy-start.13
  6.8 1.0 copy-start.14
  7.8 29.2 %copy-start.5 = (f32[1,1024,128]{2,1,0:T(8,128)S(1)}, f32[1,1024,128]{2,1,0:T(8,128)}, u32[]{:S(2)}) copy-start(f32[1,1024,128]{2,1,0:T(8,128)} %diag_ref.3) | copy-start | bytes 1572868
  17.0 2.0 %copy-start.3 = (f32[8,1024,128]{2,1,0:T(8,128)}, f32[8,1024,128]{2,1,0:T(8,128)S(1)}, u32[]{:S(2)}) copy-start(f32[8,1024,128]{2,1,0:T(8,128)S(1)} %get-tuple-element.31.t_ref) | copy-start | bytes 12582916
  19.0 1.1 copy-start.10
  20.1 16.8 %copy-start = (f32[2,1024,128]{2,1,0:T(8,128)S(1)}, f32[2,1024,128]{2,1,0:T(8,128)}, u32[]{:S(2)}) copy-start(f32[2,1024,128]{2,1,0:T(8,128)} %into_ref.5) | copy-start | bytes 3145732
  20.1 16.8 %copy-start.2 = (f32[2,1024,128]{2,1,0:T(8,128)S(1)}, f32[2,1024,128]{2,1,0:T(8,128)}, u32[]{:S(2)}) copy-start(f32[2,1024,128]{2,1,0:T(8,128)} %from_ref.3) | copy-start | bytes 3145732
  20.1 16.8 %collective-permute-start.1 = (f32[1024,128]{1,0:T(8,128)}, f32[1024,128]{1,0:T(8,128)}, u32[]{:S(2)}, u32[]{:S(2)}) collective-permute-start(f32[1024,128]{1,0:T(8,128)} %get-tuple-element.28.p_ref), channel_id=1, source_target_pairs={{32,0},{64,32},{96,64},{128,96},{160,128},{192,160},{224,192},{33,... | collective-permute-start | bytes 1572872 | tf_op jit(solution)/shard_map/ppermute | solution.py:419
  21.5 15.4 %collective-permute-start = (f32[1024,128]{1,0:T(8,128)}, f32[1024,128]{1,0:T(8,128)}, u32[]{:S(2)}, u32[]{:S(2)}) collective-permute-start(f32[1024,128]{1,0:T(8,128)} %get-tuple-element.29.m_ref), channel_id=1, source_target_pairs={{0,32},{32,64},{64,96},{96,128},{128,160},{160,192},{192,224},{1,3... | collective-permute-start | bytes 1572872 | tf_op jit(solution)/shard_map/ppermute | solution.py:419
  27.4 2.2 %copy-start.4 = (f32[8,1024,128]{2,1,0:T(8,128)S(1)}, f32[8,1024,128]{2,1,0:T(8,128)}, u32[]{:S(2)}) copy-start(f32[8,1024,128]{2,1,0:T(8,128)} %copy-done.3) | copy-start | bytes 12582916
  29.6 1.0 copy-start.7
  30.6 1.0 copy-start.9
  31.7 1.4 %copy-start.11 = (f32[22,128,128]{2,1,0:T(8,128)S(1)}, f32[22,128,128]{2,1,0:T(8,128)}, u32[]{:S(2)}) copy-start(f32[22,128,128]{2,1,0:T(8,128)} %copy-done.10) | copy-start | bytes 4325380
  40.8 22.3 %collective-permute-start.3 = (f32[1024,128]{1,0:T(8,128)S(1)}, f32[1024,128]{1,0:T(8,128)S(1)}, u32[]{:S(2)}, u32[]{:S(2)}) collective-permute-start(f32[1024,128]{1,0:T(8,128)S(1)} %get-tuple-element.36.loc_ref), channel_id=1, source_target_pairs={{32,0},{64,32},{96,64},{128,96},{160,128},{192,160},{224,192},{33,... | collective-permute-start | bytes 1572872 | tf_op jit(solution)/shard_map/ppermute | solution.py:419
  42.1 21.0 %collective-permute-start.2 = (f32[1024,128]{1,0:T(8,128)S(1)}, f32[1024,128]{1,0:T(8,128)S(1)}, u32[]{:S(2)}, u32[]{:S(2)}) collective-permute-start(f32[1024,128]{1,0:T(8,128)S(1)} %get-tuple-element.37.mm_ref), channel_id=1, source_target_pairs={{0,32},{32,64},{64,96},{96,128},{128,160},{160,192},{192,224},{1,3... | collective-permute-start | bytes 1572872 | tf_op jit(solution)/shard_map/ppermute | solution.py:419
  46.7 16.4 %collective-permute-start.6 = (f32[2,1024]{1,0:T(2,128)S(1)}, f32[2,1024]{1,0:T(2,128)S(1)}, u32[]{:S(2)}, u32[]{:S(2)}) collective-permute-start(f32[2,1024]{1,0:T(2,128)S(1)} %get-tuple-element.40), channel_id=1, source_target_pairs={{0,1},{1,2},{2,3},{4,5},{5,6},{6,7},{8,9},{9,10},{10,11},{12,13},{... | collective-permute-start | bytes 24584 | tf_op jit(solution)/shard_map/ppermute | solution.py:419
  50.5 12.7 %collective-permute-start.7 = (f32[2,1024]{1,0:T(2,128)S(1)}, f32[2,1024]{1,0:T(2,128)S(1)}, u32[]{:S(2)}, u32[]{:S(2)}) collective-permute-start(f32[2,1024]{1,0:T(2,128)S(1)} %get-tuple-element.41), channel_id=1, source_target_pairs={{1,0},{2,1},{3,2},{5,4},{6,5},{7,6},{9,8},{10,9},{11,10},{13,12},{... | collective-permute-start | bytes 24584 | tf_op jit(solution)/shard_map/ppermute | solution.py:419
  51.8 6.0 %collective-permute-start.4 = (f32[2,128]{1,0:T(2,128)S(1)}, f32[2,128]{1,0:T(2,128)S(1)}, u32[]{:S(2)}, u32[]{:S(2)}) collective-permute-start(f32[2,128]{1,0:T(2,128)S(1)} %get-tuple-element.38), channel_id=1, source_target_pairs={{0,4},{4,8},{8,12},{12,16},{16,20},{20,24},{24,28},{1,5},{5,9},{9,... | collective-permute-start | bytes 3080 | tf_op jit(solution)/shard_map/ppermute | solution.py:419
  57.7 5.4 %collective-permute-start.5 = (f32[2,128]{1,0:T(2,128)S(1)}, f32[2,128]{1,0:T(2,128)S(1)}, u32[]{:S(2)}, u32[]{:S(2)}) collective-permute-start(f32[2,128]{1,0:T(2,128)S(1)} %get-tuple-element.39), channel_id=1, source_target_pairs={{4,0},{8,4},{12,8},{16,12},{20,16},{24,20},{28,24},{5,1},{9,5},{13... | collective-permute-start | bytes 3080 | tf_op jit(solution)/shard_map/ppermute | solution.py:419
  66.9 19.2 %collective-permute-start.8 = (f32[512,128]{1,0:T(8,128)S(1)}, f32[512,128]{1,0:T(8,128)S(1)}, u32[]{:S(2)}, u32[]{:S(2)}) collective-permute-start(f32[512,128]{1,0:T(8,128)S(1)} %get-tuple-element.45), channel_id=1, source_target_pairs={{0,32},{32,64},{64,96},{96,128},{128,160},{160,192},{192,224},{1,3... | collective-permute-start | bytes 786440 | tf_op jit(solution)/shard_map/ppermute | solution.py:419
  70.6 15.5 %collective-permute-start.9 = (f32[512,128]{1,0:T(8,128)S(1)}, f32[512,128]{1,0:T(8,128)S(1)}, u32[]{:S(2)}, u32[]{:S(2)}) collective-permute-start(f32[512,128]{1,0:T(8,128)S(1)} %get-tuple-element.46.loca), channel_id=1, source_target_pairs={{32,0},{64,32},{96,64},{128,96},{160,128},{192,160},{224,192},{33,... | collective-permute-start | bytes 786440 | tf_op jit(solution)/shard_map/ppermute | solution.py:419
  71.9 14.2 %collective-permute-start.12 = (f32[2,1024]{1,0:T(2,128)S(1)}, f32[2,1024]{1,0:T(2,128)S(1)}, u32[]{:S(2)}, u32[]{:S(2)}) collective-permute-start(f32[2,1024]{1,0:T(2,128)S(1)} %get-tuple-element.50), channel_id=1, source_target_pairs={{0,1},{1,2},{2,3},{4,5},{5,6},{6,7},{8,9},{9,10},{10,11},{12,13},{... | collective-permute-start | bytes 24584 | tf_op jit(solution)/shard_map/ppermute | solution.py:419
  76.2 9.9 %collective-permute-start.13 = (f32[2,1024]{1,0:T(2,128)S(1)}, f32[2,1024]{1,0:T(2,128)S(1)}, u32[]{:S(2)}, u32[]{:S(2)}) collective-permute-start(f32[2,1024]{1,0:T(2,128)S(1)} %get-tuple-element.51), channel_id=1, source_target_pairs={{1,0},{2,1},{3,2},{5,4},{6,5},{7,6},{9,8},{10,9},{11,10},{13,12},{... | collective-permute-start | bytes 24584 | tf_op jit(solution)/shard_map/ppermute | solution.py:419
  77.5 3.2 %collective-permute-start.10 = (f32[2,128]{1,0:T(2,128)S(1)}, f32[2,128]{1,0:T(2,128)S(1)}, u32[]{:S(2)}, u32[]{:S(2)}) collective-permute-start(f32[2,128]{1,0:T(2,128)S(1)} %get-tuple-element.48), channel_id=1, source_target_pairs={{0,4},{4,8},{8,12},{12,16},{16,20},{20,24},{24,28},{1,5},{5,9},{9,... | collective-permute-start | bytes 3080 | tf_op jit(solution)/shard_map/ppermute | solution.py:419
  80.7 5.4 %collective-permute-start.11 = (f32[2,128]{1,0:T(2,128)S(1)}, f32[2,128]{1,0:T(2,128)S(1)}, u32[]{:S(2)}, u32[]{:S(2)}) collective-permute-start(f32[2,128]{1,0:T(2,128)S(1)} %get-tuple-element.49), channel_id=1, source_target_pairs={{4,0},{8,4},{12,8},{16,12},{20,16},{24,20},{28,24},{5,1},{9,5},{13... | collective-permute-start | bytes 3080 | tf_op jit(solution)/shard_map/ppermute | solution.py:419
where the time goes:
time: 123 us; the launch traced here: 122 us
  starting transfers between devices  40.2 us (33%)
  blocking collectives  30.7 us (25%)
  Pallas kernels  25.9 us (21%)
  local copies, waits for them, and re-layouts  16 us (13%)
  waiting for transfers between devices  8.42 us (7%)
    ppermute x14, starting transfers between devices, along(): return lax.ppermute(value, axis, pairs)  40.2 us
    all_to_all x1, blocking collectives, body(): gathered = lax.all_to_all(copies, AXES, 0, 0, tiled=True)  30.7 us
    unnamed x31, local copies, waits for them, and re-layouts  15.9 us
    pallas_call x1, Pallas kernels, body(): call(forward_kernel, 'forward', outside(8), [plane, plane, shape(planes,...  9.19 us
    ppermute x14, waiting for transfers between devices, along(): return lax.ppermute(value, axis, pairs)  8.42 us
    pallas_call x1, Pallas kernels, body(): call(backward_kernel, 'backward', inside(5), [shape(planes, count, width)...  3.86 us
    pallas_call x1, Pallas kernels, body(): call(first_kernel, 'first', SCALARS + inside(9), [plane] * 4 + rim_shapes...  3.85 us
    pallas_call x1, Pallas kernels, body(): call(second_kernel, 'second', SCALARS + inside(13), [plane] * 2 + [part]...  3.8 us
  transfers between devices with their start and end apart: 14, of which 4 were waited for; matrix products, arithmetic and copies ran while one was open for 0% of the time, Pallas kernels for 3%

commit v1 on v0

--- a/solution.py
+++ b/solution.py
@@ -13,10 +13,22 @@
 SCALE_ONE = 2.0**-15
 SCALE_TWO = 2.0**-30
 AXES = ("gx", "gy", "gz")
-LIMIT = 40 * 1024 * 1024
+LIMIT = 20 * 1024 * 1024
 
 F32 = jnp.float32
 BF16 = jnp.bfloat16
+
+
+BEFORE, AFTER, ABOVE, BELOW, LEFT, RIGHT = range(6)
+
+
+def neighbours():
+    spots = [(lax.axis_index(axis), lax.axis_size(axis)) for axis in AXES]
+    return [test for place, size in spots for test in (place > 0, place < size - 1)]
+
+
+def only(flags, index, value):
+    return jnp.where(flags[index], value, 0.0)
 
 
 def halves(value):
@@ -134,7 +146,7 @@
     p_ref[...] = sep[...] + link[0] * total
 
 
-def backward_kernel(t_ref, gates_ref, mats_ref, linv_ref, uinv_ref, x_ref, apply_ref, sweep_ref):
+def backward_kernel(t_ref, gates_ref, mats_ref, linv_ref, uinv_ref, x_ref, apply_ref, sweep_ref, mask_ref):
     planes = t_ref.shape[0]
     gates = gates_ref[...]
     like = t_ref.shape[1:]
@@ -167,24 +179,25 @@
     solved = product(halves(t_ref[planes - 1]), upper[planes - 1])
     x_ref[planes - 1] = solved
     for p in range(planes - 2, -1, -1):
-        gated = masked(halves(solved), -column(gates, p, like))
-        solved = product(side(halves(t_ref[p]), gated), over(upper[p], links_u[p]))
+        mask = -column(gates, p, like)
+        mask_ref[p] = mask
+        solved = product(side(halves(t_ref[p]), masked(halves(solved), mask)), over(upper[p], links_u[p]))
         x_ref[p] = solved
+    for p in range(1, planes):
+        mask_ref[planes - 2 + p] = column(gates, planes + p, like)
 
 
 def block(ref, first, count, size=128):
     return ref[0, first * size : (first + count) * size, :], ref[1, first * size : (first + count) * size, :]
 
 
-def slab(vector, following, into_ref, gates, apply_ref):
+def slab(vector, following, into_ref, mask_ref, apply_ref):
     planes = 8
-    like = vector.shape
     near = halves(into_ref[0] * vector)
     far = halves(into_ref[1] * following)
-    cuts = [None] + [column(gates, planes + p, like) for p in range(1, planes)]
-    gated = [near] + [masked(near, cuts[p]) for p in range(1, planes)]
+    gated = [near] + [masked(near, mask_ref[planes - 2 + p]) for p in range(1, planes)]
     far_end = product(side(far, gated[-1]), block(apply_ref, planes + 1, 2))
-    near_end = product(masked(far, cuts[-1]), block(apply_ref, planes, 1))
+    near_end = product(masked(far, mask_ref[2 * planes - 3]), block(apply_ref, planes, 1))
     for p in range(0, planes, 2):
         near_end = near_end + product(side(gated[p], gated[p + 1]), block(apply_ref, p, 2))
     return near_end, far_end
@@ -215,56 +228,59 @@
         column_last[index : index + 1, :] = turned[-1:]
 
 
-def rim_columns(column_low, column_high):
-    stacked = jnp.concatenate([column_low[...], column_high[...]] * 2, axis=0)
-    return jnp.transpose(stacked)
-
-
-def rim_terms(index, rows, turned, row_low, row_high, width):
+def rim_columns(flags, column_low, column_high):
+    low = (1.0 + CONVECTION) * only(flags, LEFT, column_low[...])
+    high = (1.0 - CONVECTION) * only(flags, RIGHT, column_high[...])
+    return jnp.transpose(jnp.concatenate([low, high] * 2, axis=0))
+
+
+def rim_terms(flags, index, rows, turned, row_low, row_high, width):
     start, stop, total = rows
     count = stop - start
     lane = lax.broadcasted_iota(jnp.int32, (count, width), 1)
     line = lax.broadcasted_iota(jnp.int32, (count, width), 0)
-    low = (1.0 + CONVECTION) * turned[start:stop, index : index + 1]
-    high = (1.0 - CONVECTION) * turned[start:stop, index + 2 : index + 3]
+    low = turned[start:stop, index : index + 1]
+    high = turned[start:stop, index + 2 : index + 3]
     value = jnp.where(lane == 0, low, jnp.where(lane == width - 1, high, 0.0))
     if start == 0:
-        value = value + jnp.where(line == 0, row_low[index : index + 1, :], 0.0)
+        value = value + jnp.where(line == 0, only(flags, ABOVE, row_low[index : index + 1, :]), 0.0)
     if stop == total:
-        value = value + jnp.where(line == count - 1, row_high[index : index + 1, :], 0.0)
+        value = value + jnp.where(line == count - 1, only(flags, BELOW, row_high[index : index + 1, :]), 0.0)
     return value
 
 
 def first_kernel(
-    flags, p_ref, m_ref, m_prev, p_next, into_ref, from_ref, diag_ref, gates_ref, apply_ref,
+    p_ref, m_ref, m_prev, p_next, into_ref, from_ref, diag_ref, mask_ref, apply_ref,
     k_ref, kn_ref, mm_ref, loc_ref, row_first, row_last, column_first, column_last,
 ):
-    vector = p_ref[...] + m_prev[...]
-    following = (p_next[...] + m_ref[...]) * flags[1]
+    flags = neighbours()
+    vector = p_ref[...] + only(flags, BEFORE, m_prev[...])
+    following = only(flags, AFTER, p_next[...] + m_ref[...])
     k_ref[...] = vector
     kn_ref[...] = following
     put_rims((vector, following), (row_first, row_last, column_first, column_last))
-    near, far = slab(vector, following, into_ref, gates_ref[...], apply_ref)
+    near, far = slab(vector, following, into_ref, mask_ref, apply_ref)
     mm_ref[...] = from_ref[1] * far
     loc_ref[...] = inner_stencil(vector, diag_ref[0]) - from_ref[0] * near
 
 
 def second_kernel(
-    flags, loc_ref, mm_ref, mm_prev, loc_next, row_low, row_high, column_low, column_high,
-    into_ref, from_ref, diag_ref, gates_ref, apply_ref,
+    loc_ref, mm_ref, mm_prev, loc_next, row_low, row_high, column_low, column_high,
+    into_ref, from_ref, diag_ref, mask_ref, apply_ref,
     k_ref, kn_ref, mma_ref, mmb_ref, loca_ref, locb_ref, row_first, row_last, column_first, column_last,
 ):
+    flags = neighbours()
     count, width = loc_ref.shape
     half = count // 2
-    turned = rim_columns(column_low, column_high)
+    turned = rim_columns(flags, column_low, column_high)
     rows = (0, count, count)
-    vector = loc_ref[...] - mm_prev[...] - rim_terms(0, rows, turned, row_low, row_high, width)
-    following = loc_next[...] - mm_ref[...] - rim_terms(1, rows, turned, row_low, row_high, width)
-    following = following * flags[1]
+    vector = loc_ref[...] - only(flags, BEFORE, mm_prev[...]) - rim_terms(flags, 0, rows, turned, row_low, row_high, width)
+    following = loc_next[...] - mm_ref[...] - rim_terms(flags, 1, rows, turned, row_low, row_high, width)
+    following = only(flags, AFTER, following)
     k_ref[...] = vector
     kn_ref[...] = following
     put_rims((vector, following), (row_first, row_last, column_first, column_last))
-    near, far = slab(vector, following, into_ref, gates_ref[...], apply_ref)
+    near, far = slab(vector, following, into_ref, mask_ref, apply_ref)
     sent = from_ref[1] * far
     mma_ref[...] = sent[:half]
     mmb_ref[...] = sent[half:]
@@ -274,32 +290,35 @@
 
 
 def sums_kernel(
-    flags, k0, k0n, k1, k1n, mma, mmb_prev, loca, locb, loca_next, row_low, row_high, column_low, column_high,
+    k0, k0n, k1, k1n, mma, mmb_prev, loca, locb, loca_next, row_low, row_high, column_low, column_high, x0_ref, x1_ref,
     out_ref,
 ):
+    flags = neighbours()
     count, width = k0.shape
     half = count // 2
-    turned = rim_columns(column_low, column_high)
+    turned = rim_columns(flags, column_low, column_high)
     top, bottom = (0, half, count), (half, count, count)
-    own_low = loca[...] - rim_terms(0, top, turned, row_low, row_high, width)
-    own_high = locb[...] - mmb_prev[...] - rim_terms(0, bottom, turned, row_low, row_high, width)
-    next_low = loca_next[...] - mma[...] - rim_terms(1, top, turned, row_low, row_high, width)
+    own_low = loca[...] - rim_terms(flags, 0, top, turned, row_low, row_high, width)
+    own_high = locb[...] - only(flags, BEFORE, mmb_prev[...]) - rim_terms(flags, 0, bottom, turned, row_low, row_high, width)
+    next_low = loca_next[...] - mma[...] - rim_terms(flags, 1, top, turned, row_low, row_high, width)
     groups = (
-        (k0[half:], k1[half:] * SCALE_ONE, own_high * SCALE_TWO, None),
-        (k0n[:half], k1n[:half] * SCALE_ONE, next_low * SCALE_TWO, flags[1]),
-        (k0[:half], k1[:half] * SCALE_ONE, own_low * SCALE_TWO, flags[0]),
+        (k0[half:], k1[half:] * SCALE_ONE, own_high * SCALE_TWO),
+        (k0n[:half], k1n[:half] * SCALE_ONE, only(flags, AFTER, next_low) * SCALE_TWO),
+        (k0[:half], k1[:half] * SCALE_ONE, own_low * SCALE_TWO),
     )
     totals = [0.0] * 6
-    for zero, one, two, weight in groups:
+    for ordinal, (zero, one, two) in enumerate(groups):
         pairs = ((zero, zero), (zero, one), (one, one), (zero, two), (one, two), (two, two))
         for index, (left, right) in enumerate(pairs):
             value = jnp.sum((left * right).reshape(half // 8, 8, width), axis=0)
-            totals[index] = totals[index] + (value if weight is None else value * weight)
+            if ordinal == 2:
+                value = jnp.where(flags[BEFORE], 0.0, value)
+            totals[index] = totals[index] + value
     lane = lax.broadcasted_iota(jnp.int32, (1, width), 1)
     line = jnp.zeros((1, width), F32)
     for index in range(6):
         line = jnp.where(lane == index, jnp.sum(totals[index]), line)
-    out_ref[...] = line
+    out_ref[...] = jnp.broadcast_to(line, out_ref.shape)
 
 
 def weights(sums):
@@ -341,35 +360,35 @@
     return weight_one / beta - scaled_two * delta, scaled_two
 
 
-def final_kernel(
-    gathered, k0, k0n, k1, k1n, into_ref, gates_ref, apply_ref, sweep_ref, x_ref,
-    out_hbm, sep_hbm, out, sep, sems,
-):
+def sweep_kernel(k, kn, into_ref, mask_ref, apply_ref, sweep_ref, x_ref):
+    planes = x_ref.shape[0]
+    near = halves(into_ref[0] * k[...])
+    far = halves(into_ref[1] * kn[...])
+    running = None
+    for p in range(planes - 1, -1, -1):
+        gated = near if p == 0 else masked(near, mask_ref[planes - 2 + p])
+        if running is None:
+            running = product(side(far, gated), block(apply_ref, planes + 1, 2))
+        else:
+            other = masked(halves(running), mask_ref[p])
+            running = product(side(gated, other), block(sweep_ref, 2 * p, 2))
+        x_ref[p] = running
+
+
+def final_kernel(gathered, k0, k1, x_ref, x0_ref, x1_ref, out_hbm, sep_hbm, out, sep, sems):
     planes = x_ref.shape[0]
     line = jnp.sum(gathered[...], axis=0, keepdims=True)
     lane = lax.broadcasted_iota(jnp.int32, line.shape, 1)
     sums = [jnp.sum(jnp.where(lane == index, line, 0.0), axis=1, keepdims=True) for index in range(6)]
     one, two = weights(sums)
-    vector = one * k0[...] + two * k1[...]
-    following = one * k0n[...] + two * k1n[...]
-    sep[...] = vector
-    copies = [pltpu.make_async_copy(sep, sep_hbm.at[0], sems.at[planes])]
-    copies[0].start()
-    gates = gates_ref[...]
-    like = vector.shape
-    near = halves(into_ref[0] * vector)
-    far = halves(into_ref[1] * following)
-    running = None
-    for p in range(planes - 1, -1, -1):
-        gated = near if p == 0 else masked(near, column(gates, planes + p, like))
-        if running is None:
-            running = product(side(far, gated), block(apply_ref, planes + 1, 2))
-        else:
-            other = masked(halves(running), -column(gates, p, like))
-            running = product(side(gated, other), block(sweep_ref, 2 * p, 2))
-        out[p] = x_ref[p] + running
+    copies = []
+    for p in range(planes):
+        out[p] = x_ref[p] + (one * x0_ref[p] + two * x1_ref[p])
         copies.append(pltpu.make_async_copy(out.at[p], out_hbm.at[p], sems.at[p]))
         copies[-1].start()
+    sep[...] = one * k0[...] + two * k1[...]
+    copies.append(pltpu.make_async_copy(sep, sep_hbm.at[0], sems.at[planes]))
+    copies[-1].start()
     for copy in copies:
         copy.wait()
 
@@ -378,11 +397,8 @@
     return [pl.BlockSpec(memory_space=pltpu.VMEM)] * count
 
 
-def outside(count):
-    return [pl.BlockSpec(memory_space=pl.ANY)] * count
-
-
-SCALARS = [pl.BlockSpec(memory_space=pltpu.SMEM)]
+def outside(count, space=pl.ANY):
+    return [pl.BlockSpec(memory_space=space)] * count
 
 
 def shape(*sizes, dtype=F32):
@@ -408,15 +424,12 @@
     planes, count, width = rhs_interior.shape
     half = count // 2
     slabs, blocks, lines = (lax.axis_size(axis) for axis in AXES)
-    place = lax.axis_index("gx")
-    flags = jnp.stack([place == 0, place < slabs - 1]).astype(F32)
     plane = shape(count, width)
     dense = 2 * 2 * count * width * width
 
     def along(value, axis, by):
         size = lax.axis_size(axis)
-        pairs = [(i, i + by) for i in range(size) if 0 <= i + by < size]
-        return lax.ppermute(value, axis, pairs)
+        return lax.ppermute(value, axis, [(i, (i + by) % size) for i in range(size)])
 
     def rims(row_first, row_last, column_first, column_last):
         return (
@@ -431,7 +444,7 @@
     m, p, t, gates, mats = call(
         forward_kernel,
         "forward",
-        outside(8),
+        outside(8, pltpu.HBM),
         [plane, plane, shape(planes, count, width), shape(count, 2 * planes), shape(3 * planes - 2, width, width)],
         inside(5),
         [
@@ -447,10 +460,13 @@
         ],
         flops=dense * 24,
         moved=12 << 20,
-    )(rhs_interior, lower_inv, lower_off, upper_inv, upper_off, coupling, rhs_sep, link_from)
+    )(*(
+        pltpu.with_memory_space_constraint(array, pltpu.HBM)
+        for array in (rhs_interior, lower_inv, lower_off, upper_inv, upper_off, coupling, rhs_sep, link_from)
+    ))
     m_prev = along(m, "gx", 1)
     p_next = along(p, "gx", -1)
-    x, applied, swept = call(
+    x, applied, swept, masks = call(
         backward_kernel,
         "backward",
         inside(5),
@@ -458,51 +474,65 @@
             shape(planes, count, width),
             shape(2, (planes + 3) * width, width, dtype=BF16),
             shape(2, (2 * planes - 2) * width, width, dtype=BF16),
+            shape(2 * planes - 2, count, width, dtype=BF16),
         ],
-        inside(3),
+        inside(4),
         flops=dense * 20,
         moved=12 << 20,
     )(t, gates, mats, lower_inv, upper_inv)
     k0, k0n, mm, loc, *edges = call(
         first_kernel,
         "first",
-        SCALARS + inside(9),
+        inside(9),
         [plane] * 4 + rim_shapes,
         inside(8),
         flops=dense * 11,
         moved=4 << 20,
-    )(flags, p, m, m_prev, p_next, link_into, link_from, sep_diag, gates, applied)
+    )(p, m, m_prev, p_next, link_into, link_from, sep_diag, masks, applied)
     mm_prev = along(mm, "gx", 1)
     loc_next = along(loc, "gx", -1)
     arrived = rims(*edges)
+
+    def swept_field(name, k, kn):
+        return call(
+            sweep_kernel,
+            name,
+            inside(6),
+            shape(planes, count, width),
+            pl.BlockSpec(memory_space=pltpu.VMEM),
+            flops=dense * 16,
+            moved=8 << 20,
+        )(k, kn, link_into, masks, applied, swept)
+
+    x0 = swept_field("sweep_first", k0, k0n)
     part = shape(half, width)
     k1, k1n, mma, mmb, loca, locb, *edges = call(
         second_kernel,
         "second",
-        SCALARS + inside(13),
+        inside(13),
         [plane] * 2 + [part] * 4 + rim_shapes,
         inside(10),
         flops=dense * 11,
         moved=4 << 20,
-    )(flags, loc, mm, mm_prev, loc_next, *arrived, link_into, link_from, sep_diag, gates, applied)
+    )(loc, mm, mm_prev, loc_next, *arrived, link_into, link_from, sep_diag, masks, applied)
     mmb_prev = along(mmb, "gx", 1)
     loca_next = along(loca, "gx", -1)
     arrived = rims(*edges)
+    x1 = swept_field("sweep_second", k1, k1n)
     line = call(
         sums_kernel,
         "sums",
-        SCALARS + inside(13),
-        shape(1, width),
+        inside(13) + outside(2),
+        shape(slabs * blocks * lines, width),
         pl.BlockSpec(memory_space=pltpu.VMEM),
         flops=dense,
         moved=4 << 20,
-    )(flags, k0, k0n, k1, k1n, mma, mmb_prev, loca, locb, loca_next, *arrived)
-    copies = jnp.broadcast_to(line, (slabs * blocks * lines, width))
-    gathered = lax.all_to_all(copies, AXES, 0, 0, tiled=True)
+    )(k0, k0n, k1, k1n, mma, mmb_prev, loca, locb, loca_next, *arrived, x0, x1)
+    gathered = lax.all_to_all(line, AXES, 0, 0, tiled=True)
     interior, separator = call(
         final_kernel,
         "final",
-        inside(10),
+        inside(6),
         [shape(planes, count, width), shape(1, count, width)],
         outside(2),
         [
@@ -510,9 +540,9 @@
             pltpu.VMEM((count, width), F32),
             pltpu.SemaphoreType.DMA((planes + 1,)),
         ],
-        flops=dense * 16,
-        moved=12 << 20,
-    )(gathered, k0, k0n, k1, k1n, link_into, gates, applied, swept, x)
+        flops=dense,
+        moved=16 << 20,
+    )(gathered, k0, k1, x, x0, x1)
     return interior, separator
 
 

time: 123 us -> 88.2 us (0.72)
  local copies, waits for them, and re-layouts: 16 us -> 1.49 us
  starting transfers between devices: 40.2 us -> 27.6 us
  blocking collectives: 30.7 us -> 22.1 us
  waiting for transfers between devices: 8.42 us -> 10.2 us
    unnamed x31 -> x11, local copies, waits for them, and re-layouts: 15.9 us -> 1.49 us
    ppermute x14, starting transfers between devices: 40.2 us -> 27.6 us  [along(): lax.ppermute(value, axis, [(i, (i + by) % size) for i in range(size)])]
    all_to_all x1, blocking collectives: 30.7 us -> 22.1 us  [body(): gathered = lax.all_to_all(line, AXES, 0, 0, tiled=True)]
    ppermute x14, waiting for transfers between devices: 8.42 us -> 10.2 us  [along(): lax.ppermute(value, axis, [(i, (i + by) % size) for i in range(size)])]
    pallas_call x5 -> x7, Pallas kernels: 22 us -> 21.8 us  [the longest x1 8.92 us: body(): call(forward_kernel, 'forward', outside(8, pltpu.HBM), [plane, plane, sha...]
  transfers between devices with their start and end apart: 14 -> 14, of which waited for: 4 -> 4; matrix products, arithmetic and copies ran while one was open for 0% -> 0% of each run, Pallas kernels for 3% -> 10%
where the time goes in v1:
time: 88.2 us; the launch traced here: 88.1 us
  starting transfers between devices  27.6 us (31%)
  Pallas kernels  25.8 us (29%)
  blocking collectives  22.1 us (25%)
  waiting for transfers between devices  10.2 us (12%)
  local copies, waits for them, and re-layouts  1.49 us (2%)
  between operations  0.95 us (1%)
    ppermute x14, starting transfers between devices, along(): lax.ppermute(value, axis, [(i, (i + by) % size) for i in range(size)])  27.6 us
    all_to_all x1, blocking collectives, body(): gathered = lax.all_to_all(line, AXES, 0, 0, tiled=True)  22.1 us
    ppermute x14, waiting for transfers between devices, along(): lax.ppermute(value, axis, [(i, (i + by) % size) for i in range(size)])  10.2 us
    pallas_call x1, Pallas kernels, body(): call(forward_kernel, 'forward', outside(8, pltpu.HBM), [plane, plane, sha...  8.92 us
    pallas_call x2, Pallas kernels, swept_field(): call(sweep_kernel, name, inside(6), shape(planes, count, width), pl.Block...  4.72 us
    pallas_call x1, Pallas kernels, body(): call(backward_kernel, 'backward', inside(5), [shape(planes, count, width)...  4.02 us
    pallas_call x1, Pallas kernels, body(): call(second_kernel, 'second', inside(13), [plane] * 2 + [part] * 4 + rim_...  2.71 us
    pallas_call x1, Pallas kernels, body(): call(final_kernel, 'final', inside(6), [shape(planes, count, width), shap...  2.59 us
  transfers between devices with their start and end apart: 14, of which 4 were waited for; matrix products, arithmetic and copies ran while one was open for 0% of the time, Pallas kernels for 10%

profile of v1, /device:TPU:1, one launch (start us, length us, event | category | flops | bytes accessed | tf_op | source)
XLA Modules:
  0.0 88.1 jit_solution(12719177740657831608)
XLA Ops:
  0.6 0.0 copy-start.3
  0.6 0.0 copy-start.4
  0.7 1.5 %copy.13.coupling_hbm = s32[1,7,1024]{2,1,0:T(8,128)} copy(s32[1,7,1024]{2,0,1:T(1,128)} %param.19) | data formatting | bytes 57344 | tf_op args[9]
  2.1 8.9 %forward.1 = (f32[1024,128]{1,0:T(8,128)S(1)}, f32[1024,128]{1,0:T(8,128)S(1)}, f32[8,1024,128]{2,1,0:T(8,128)S(1)}, f32[1024,16]{1,0:T(8,128)S(1)}, f32[22,128,128]{2,1,0:T(8,128)S(1)}) custom-call(f32[8,1024,128]{2,1,0:T(8,128)} %rhs_hbm.1, f32[8,1,1,128,128]{4,3,2,1,0:T(8,128)} %linv_ref.1, f32[7,1,1,128,128]{4,3,2,1,0:T(8,128)} %loff_hbm.1, ...), custom_call_target="tpu_custom_call" | custom-call | flops 1610612736 | bytes 12582912 | tf_op jit(solution)/shard_map/forward/pallas_call | solution.py:444
  11.0 0.0 copy-start
  11.0 0.0 copy-start.1
  11.1 0.0 copy-start.2
  11.1 2.5 %collective-permute-start = (f32[1024,128]{1,0:T(8,128)S(1)}, f32[1024,128]{1,0:T(8,128)S(1)}, u32[]{:S(2)}, u32[]{:S(2)}) collective-permute-start(f32[1024,128]{1,0:T(8,128)S(1)} %get-tuple-element.30.m_ref), channel_id=1, source_target_pairs={{0,32},{32,64},{64,96},{96,128},{128,160},{160,192},{192,224},{224... | collective-permute-start | bytes 1572872 | tf_op jit(solution)/shard_map/ppermute | solution.py:432
  13.6 4.2 %collective-permute-start.1 = (f32[1024,128]{1,0:T(8,128)S(1)}, f32[1024,128]{1,0:T(8,128)S(1)}, u32[]{:S(2)}, u32[]{:S(2)}) collective-permute-start(f32[1024,128]{1,0:T(8,128)S(1)} %get-tuple-element.29.p_ref), channel_id=1, source_target_pairs={{0,224},{32,0},{64,32},{96,64},{128,96},{160,128},{192,160},{224,1... | collective-permute-start | bytes 1572872 | tf_op jit(solution)/shard_map/ppermute | solution.py:432
  17.8 0.0 copy-done.3
  17.8 0.0 copy-done.4
  17.8 4.0 %backward.1 = (f32[8,1024,128]{2,1,0:T(8,128)S(1)}, bf16[2,1408,128]{2,1,0:T(8,128)(2,1)S(1)}, bf16[2,1792,128]{2,1,0:T(8,128)(2,1)S(1)}, bf16[14,1024,128]{2,1,0:T(8,128)(2,1)S(1)}) custom-call(f32[8,1024,128]{2,1,0:T(8,128)S(1)} %get-tuple-element.31.t_ref, f32[1024,16]{1,0:T(8,128)S(1)} %get-tuple-element.32.gates_ref, ...), custom_call_target="tpu_custom_call" | custom-call | flops 1342177280 | bytes 12582912 | tf_op jit(solution)/shard_map/backward/pallas_call | solution.py:469
  21.9 7.4 %collective-permute-done.m_prev = f32[1024,128]{1,0:T(8,128)S(1)} collective-permute-done((f32[1024,128]{1,0:T(8,128)S(1)}, f32[1024,128]{1,0:T(8,128)S(1)}, u32[]{:S(2)}, u32[]{:S(2)}) %collective-permute-start) | collective-permute-done | bytes 524320 | tf_op jit(solution)/shard_map/ppermute | solution.py:432
  29.2 0.0 collective-permute-done.1.p_next
  29.2 0.0 copy-done
  29.2 0.0 copy-done.1
  29.2 0.0 copy-done.2
  29.2 1.8 %first.1 = (f32[1024,128]{1,0:T(8,128)S(1)}, f32[1024,128]{1,0:T(8,128)S(1)}, f32[1024,128]{1,0:T(8,128)S(1)}, f32[1024,128]{1,0:T(8,128)S(1)}, f32[2,128]{1,0:T...) custom-call(f32[1024,128]{1,0:T(8,128)S(1)} %get-tuple-element.29.p_ref, ...), custom_call_target="tpu_custom_call" | custom-call | flops 738197504 | bytes 4194304 | tf_op jit(solution)/shard_map/first/pallas_call | solution.py:483
  31.1 0.1 collective-permute-start.2
  31.2 2.7 %collective-permute-start.3 = (f32[1024,128]{1,0:T(8,128)S(1)}, f32[1024,128]{1,0:T(8,128)S(1)}, u32[]{:S(2)}, u32[]{:S(2)}) collective-permute-start(f32[1024,128]{1,0:T(8,128)S(1)} %get-tuple-element.38.loc_ref), channel_id=1, source_target_pairs={{0,224},{32,0},{64,32},{96,64},{128,96},{160,128},{192,160},{224,1... | collective-permute-start | bytes 1572872 | tf_op jit(solution)/shard_map/ppermute | solution.py:432
  33.9 1.3 %collective-permute-start.6 = (f32[2,1024]{1,0:T(2,128)S(1)}, f32[2,1024]{1,0:T(2,128)S(1)}, u32[]{:S(2)}, u32[]{:S(2)}) collective-permute-start(f32[2,1024]{1,0:T(2,128)S(1)} %get-tuple-element.42), channel_id=1, source_target_pairs={{0,1},{1,2},{2,3},{3,0},{4,5},{5,6},{6,7},{7,4},{8,9},{9,10},{10,1... | collective-permute-start | bytes 24584 | tf_op jit(solution)/shard_map/ppermute | solution.py:432
  35.1 1.4 %collective-permute-start.7 = (f32[2,1024]{1,0:T(2,128)S(1)}, f32[2,1024]{1,0:T(2,128)S(1)}, u32[]{:S(2)}, u32[]{:S(2)}) collective-permute-start(f32[2,1024]{1,0:T(2,128)S(1)} %get-tuple-element.43), channel_id=1, source_target_pairs={{0,3},{1,0},{2,1},{3,2},{4,7},{5,4},{6,5},{7,6},{8,11},{9,8},{10,9... | collective-permute-start | bytes 24584 | tf_op jit(solution)/shard_map/ppermute | solution.py:432
  36.6 3.4 %collective-permute-start.4 = (f32[2,128]{1,0:T(2,128)S(1)}, f32[2,128]{1,0:T(2,128)S(1)}, u32[]{:S(2)}, u32[]{:S(2)}) collective-permute-start(f32[2,128]{1,0:T(2,128)S(1)} %get-tuple-element.40), channel_id=1, source_target_pairs={{0,4},{4,8},{8,12},{12,16},{16,20},{20,24},{24,28},{28,0},{1,5},{5... | collective-permute-start | bytes 3080 | tf_op jit(solution)/shard_map/ppermute | solution.py:432
  40.0 0.7 collective-permute-done.4.row_low
  40.7 2.4 %collective-permute-start.5 = (f32[2,128]{1,0:T(2,128)S(1)}, f32[2,128]{1,0:T(2,128)S(1)}, u32[]{:S(2)}, u32[]{:S(2)}) collective-permute-start(f32[2,128]{1,0:T(2,128)S(1)} %get-tuple-element.41), channel_id=1, source_target_pairs={{0,28},{4,0},{8,4},{12,8},{16,12},{20,16},{24,20},{28,24},{1,29},{... | collective-permute-start | bytes 3080 | tf_op jit(solution)/shard_map/ppermute | solution.py:432
  43.1 1.4 %collective-permute-done.5.row_high = f32[2,128]{1,0:T(2,128)S(1)} collective-permute-done((f32[2,128]{1,0:T(2,128)S(1)}, f32[2,128]{1,0:T(2,128)S(1)}, u32[]{:S(2)}, u32[]{:S(2)}) %collective-permute-start.5) | collective-permute-done | bytes 1056 | tf_op jit(solution)/shard_map/ppermute | solution.py:432
  44.5 0.0 collective-permute-done.6.column_low
  44.6 0.0 collective-permute-done.7.column_high
  44.6 0.0 collective-permute-done.2.mm_prev
  44.6 0.0 collective-permute-done.3.loc_next
  44.6 2.7 %second.1 = (f32[1024,128]{1,0:T(8,128)S(1)}, f32[1024,128]{1,0:T(8,128)S(1)}, f32[512,128]{1,0:T(8,128)S(1)}, f32[512,128]{1,0:T(8,128)S(1)}, f32[512,128]{1,0:...) custom-call(f32[1024,128]{1,0:T(8,128)S(1)} %get-tuple-element.38.lo, ...), custom_call_target="tpu_custom_call" | custom-call | flops 738197504 | bytes 4194304 | tf_op jit(solution)/shard_map/second/pallas_call | solution.py:509
  47.3 0.9 %collective-permute-start.8 = (f32[512,128]{1,0:T(8,128)S(1)}, f32[512,128]{1,0:T(8,128)S(1)}, u32[]{:S(2)}, u32[]{:S(2)}) collective-permute-start(f32[512,128]{1,0:T(8,128)S(1)} %get-tuple-element.47), channel_id=1, source_target_pairs={{0,32},{32,64},{64,96},{96,128},{128,160},{160,192},{192,224},{224... | collective-permute-start | bytes 786440 | tf_op jit(solution)/shard_map/ppermute | solution.py:432
  48.2 1.8 %collective-permute-start.9 = (f32[512,128]{1,0:T(8,128)S(1)}, f32[512,128]{1,0:T(8,128)S(1)}, u32[]{:S(2)}, u32[]{:S(2)}) collective-permute-start(f32[512,128]{1,0:T(8,128)S(1)} %get-tuple-element.48.loca), channel_id=1, source_target_pairs={{0,224},{32,0},{64,32},{96,64},{128,96},{160,128},{192,160},{224,1... | collective-permute-start | bytes 786440 | tf_op jit(solution)/shard_map/ppermute | solution.py:432
  50.0 3.8 %collective-permute-start.10 = (f32[2,128]{1,0:T(2,128)S(1)}, f32[2,128]{1,0:T(2,128)S(1)}, u32[]{:S(2)}, u32[]{:S(2)}) collective-permute-start(f32[2,128]{1,0:T(2,128)S(1)} %get-tuple-element.50), channel_id=1, source_target_pairs={{0,4},{4,8},{8,12},{12,16},{16,20},{20,24},{24,28},{28,0},{1,5},{5... | collective-permute-start | bytes 3080 | tf_op jit(solution)/shard_map/ppermute | solution.py:432
  53.9 2.4 %sweep_first.1.x0_ref = f32[8,1024,128]{2,1,0:T(8,128)S(1)} custom-call(f32[1024,128]{1,0:T(8,128)S(1)} %get-tuple-element.36.k.k0, f32[1024,128]{1,0:T(8,128)S(1)} %get-tuple-element.37.kn.k0n, f32[2,1024,128]{2,1,0:T(8,128)S(1)} %copy-done, bf16[14,1024,128]{2,1,0:T(8,128)(2,1)S(1)} %get-tuple-element.34.mask_ref, ...), custom_call_target="tpu_custom_call" | custom-call | flops 1073741824 | bytes 8388608 | tf_op jit(solution)/shard_map/sweep_first/pallas_call | solution.py:497
  56.2 1.4 %collective-permute-start.12 = (f32[2,1024]{1,0:T(2,128)S(1)}, f32[2,1024]{1,0:T(2,128)S(1)}, u32[]{:S(2)}, u32[]{:S(2)}) collective-permute-start(f32[2,1024]{1,0:T(2,128)S(1)} %get-tuple-element.52), channel_id=1, source_target_pairs={{0,1},{1,2},{2,3},{3,0},{4,5},{5,6},{6,7},{7,4},{8,9},{9,10},{10,1... | collective-permute-start | bytes 24584 | tf_op jit(solution)/shard_map/ppermute | solution.py:432
  57.6 1.5 %collective-permute-start.13 = (f32[2,1024]{1,0:T(2,128)S(1)}, f32[2,1024]{1,0:T(2,128)S(1)}, u32[]{:S(2)}, u32[]{:S(2)}) collective-permute-start(f32[2,1024]{1,0:T(2,128)S(1)} %get-tuple-element.53), channel_id=1, source_target_pairs={{0,3},{1,0},{2,1},{3,2},{4,7},{5,4},{6,5},{7,6},{8,11},{9,8},{10,9... | collective-permute-start | bytes 24584 | tf_op jit(solution)/shard_map/ppermute | solution.py:432
  59.2 0.0 collective-permute-done.10.row_low
  59.2 0.0 collective-permute-start.11
  59.2 2.4 %sweep_second.1.x1_ref = f32[8,1024,128]{2,1,0:T(8,128)S(1)} custom-call(f32[1024,128]{1,0:T(8,128)S(1)} %get-tuple-element.44.k.k1, f32[1024,128]{1,0:T(8,128)S(1)} %get-tuple-element.45.kn.k1n, f32[2,1024,128]{2,1,0:T(8,128)S(1)} %copy-done, bf16[14,1024,128]{2,1,0:T(8,128)(2,1)S(1)} %get-tuple-element.34.mask_ref, ...), custom_call_target="tpu_custom_call" | custom-call | flops 1073741824 | bytes 8388608 | tf_op jit(solution)/shard_map/sweep_second/pallas_call | solution.py:497
  61.5 0.6 collective-permute-done.11.row_high
  62.2 0.0 collective-permute-done.12.column_low
  62.2 0.0 collective-permute-done.13.column_high
  62.2 0.0 collective-permute-done.8.mmb_prev
  62.2 0.0 collective-permute-done.9.loca_next
  62.2 1.0 %sums.1 = f32[256,128]{1,0:T(8,128)S(1)} custom-call(f32[1024,128]{1,0:T(8,128)S(1)} %get-tuple-element.36.k.k0, f32[1024,128]{1,0:T(8,128)S(1)} %get-tuple-element.37.kn.k0n, f32[1024,128]{1,0:T(8,128)S(1)} %get-tuple-element.44.k.k1, f32[1024,128]{1,0:T(8,128)S(1)} %get-tuple-element.45.kn.k1n, f32[512,128]{1,0:T(8,128)S(1)} %get-tuple-element.46.mma, ...), custom_call_target="tpu_custom_call" | custom-call | flops 67108864 | bytes 4194304 | tf_op jit(solution)/shard_map/sums/pallas_call | solution.py:522
  63.2 22.1 %all_to_all.11 = f32[256,1,128]{2,1,0:T(1,128)S(1)} all-to-all(f32[256,1,128]{2,1,0:T(1,128)S(1)} %bitcast.4), channel_id=1, replica_groups=mesh['gx'=8,'gy'=8,'gz'=4] {'gx','gy','gz'}, dimensions={0} | all-to-all | bytes 262144 | tf_op jit(solution)/shard_map/all_to_all | solution.py:531
  85.3 2.6 %final.1 = (f32[8,1024,128]{2,1,0:T(8,128)}, f32[1,1024,128]{2,1,0:T(8,128)}) custom-call(f32[256,128]{1,0:T(8,128)S(1)} %bitcast.5, f32[1024,128]{1,0:T(8,128)S(1)} %get-tuple-element.36.k.k0, f32[1024,128]{1,0:T(8,128)S(1)} %get-tuple-element.44.k.k1, f32[8,1024,128]{2,1,0:T(8,128)S(1)} %get-tuple-element.55.x_ref, f32[8,1024,128]{2,1,0:T(8,128)S(1)} %sweep_first.1.x0_ref, ...), custom_call_target="tpu_custom_call" | custom-call | flops 67108864 | bytes 16777216 | tf_op jit(solution)/shard_map/final/pallas_call | solution.py:532
Async XLA Ops:
  0.6 17.2 %copy-start.3 = (f32[8,1,1,128,128]{4,3,2,1,0:T(8,128)S(1)}, f32[8,1,1,128,128]{4,3,2,1,0:T(8,128)}, u32[]{:S(2)}) copy-start(f32[8,1,1,128,128]{4,3,2,1,0:T(8,128)} %linv_ref.1) | copy-start | bytes 1572868
  0.6 17.2 %copy-start.4 = (f32[8,1,1,128,128]{4,3,2,1,0:T(8,128)S(1)}, f32[8,1,1,128,128]{4,3,2,1,0:T(8,128)}, u32[]{:S(2)}) copy-start(f32[8,1,1,128,128]{4,3,2,1,0:T(8,128)} %uinv_ref.1) | copy-start | bytes 1572868
  11.0 18.2 %copy-start = (f32[2,1024,128]{2,1,0:T(8,128)S(1)}, f32[2,1024,128]{2,1,0:T(8,128)}, u32[]{:S(2)}) copy-start(f32[2,1024,128]{2,1,0:T(8,128)} %into_ref.7) | copy-start | bytes 3145732
  11.0 18.2 %copy-start.1 = (f32[2,1024,128]{2,1,0:T(8,128)S(1)}, f32[2,1024,128]{2,1,0:T(8,128)}, u32[]{:S(2)}) copy-start(f32[2,1024,128]{2,1,0:T(8,128)} %from_ref.3) | copy-start | bytes 3145732
  11.1 18.2 %copy-start.2 = (f32[1,1024,128]{2,1,0:T(8,128)S(1)}, f32[1,1024,128]{2,1,0:T(8,128)}, u32[]{:S(2)}) copy-start(f32[1,1024,128]{2,1,0:T(8,128)} %diag_ref.3) | copy-start | bytes 1572868
  11.1 18.1 %collective-permute-start = (f32[1024,128]{1,0:T(8,128)S(1)}, f32[1024,128]{1,0:T(8,128)S(1)}, u32[]{:S(2)}, u32[]{:S(2)}) collective-permute-start(f32[1024,128]{1,0:T(8,128)S(1)} %get-tuple-element.30.m_ref), channel_id=1, source_target_pairs={{0,32},{32,64},{64,96},{96,128},{128,160},{160,192},{192,224},{224... | collective-permute-start | bytes 1572872 | tf_op jit(solution)/shard_map/ppermute | solution.py:432
  13.6 15.6 %collective-permute-start.1 = (f32[1024,128]{1,0:T(8,128)S(1)}, f32[1024,128]{1,0:T(8,128)S(1)}, u32[]{:S(2)}, u32[]{:S(2)}) collective-permute-start(f32[1024,128]{1,0:T(8,128)S(1)} %get-tuple-element.29.p_ref), channel_id=1, source_target_pairs={{0,224},{32,0},{64,32},{96,64},{128,96},{160,128},{192,160},{224,1... | collective-permute-start | bytes 1572872 | tf_op jit(solution)/shard_map/ppermute | solution.py:432
  31.1 13.5 %collective-permute-start.2 = (f32[1024,128]{1,0:T(8,128)S(1)}, f32[1024,128]{1,0:T(8,128)S(1)}, u32[]{:S(2)}, u32[]{:S(2)}) collective-permute-start(f32[1024,128]{1,0:T(8,128)S(1)} %get-tuple-element.39.mm_ref), channel_id=1, source_target_pairs={{0,32},{32,64},{64,96},{96,128},{128,160},{160,192},{192,224},{224... | collective-permute-start | bytes 1572872 | tf_op jit(solution)/shard_map/ppermute | solution.py:432
  31.2 13.4 %collective-permute-start.3 = (f32[1024,128]{1,0:T(8,128)S(1)}, f32[1024,128]{1,0:T(8,128)S(1)}, u32[]{:S(2)}, u32[]{:S(2)}) collective-permute-start(f32[1024,128]{1,0:T(8,128)S(1)} %get-tuple-element.38.loc_ref), channel_id=1, source_target_pairs={{0,224},{32,0},{64,32},{96,64},{128,96},{160,128},{192,160},{224,1... | collective-permute-start | bytes 1572872 | tf_op jit(solution)/shard_map/ppermute | solution.py:432
  33.9 10.7 %collective-permute-start.6 = (f32[2,1024]{1,0:T(2,128)S(1)}, f32[2,1024]{1,0:T(2,128)S(1)}, u32[]{:S(2)}, u32[]{:S(2)}) collective-permute-start(f32[2,1024]{1,0:T(2,128)S(1)} %get-tuple-element.42), channel_id=1, source_target_pairs={{0,1},{1,2},{2,3},{3,0},{4,5},{5,6},{6,7},{7,4},{8,9},{9,10},{10,1... | collective-permute-start | bytes 24584 | tf_op jit(solution)/shard_map/ppermute | solution.py:432
  35.1 9.4 %collective-permute-start.7 = (f32[2,1024]{1,0:T(2,128)S(1)}, f32[2,1024]{1,0:T(2,128)S(1)}, u32[]{:S(2)}, u32[]{:S(2)}) collective-permute-start(f32[2,1024]{1,0:T(2,128)S(1)} %get-tuple-element.43), channel_id=1, source_target_pairs={{0,3},{1,0},{2,1},{3,2},{4,7},{5,4},{6,5},{7,6},{8,11},{9,8},{10,9... | collective-permute-start | bytes 24584 | tf_op jit(solution)/shard_map/ppermute | solution.py:432
  36.6 4.2 %collective-permute-start.4 = (f32[2,128]{1,0:T(2,128)S(1)}, f32[2,128]{1,0:T(2,128)S(1)}, u32[]{:S(2)}, u32[]{:S(2)}) collective-permute-start(f32[2,128]{1,0:T(2,128)S(1)} %get-tuple-element.40), channel_id=1, source_target_pairs={{0,4},{4,8},{8,12},{12,16},{16,20},{20,24},{24,28},{28,0},{1,5},{5... | collective-permute-start | bytes 3080 | tf_op jit(solution)/shard_map/ppermute | solution.py:432
  40.7 3.8 %collective-permute-start.5 = (f32[2,128]{1,0:T(2,128)S(1)}, f32[2,128]{1,0:T(2,128)S(1)}, u32[]{:S(2)}, u32[]{:S(2)}) collective-permute-start(f32[2,128]{1,0:T(2,128)S(1)} %get-tuple-element.41), channel_id=1, source_target_pairs={{0,28},{4,0},{8,4},{12,8},{16,12},{20,16},{24,20},{28,24},{1,29},{... | collective-permute-start | bytes 3080 | tf_op jit(solution)/shard_map/ppermute | solution.py:432
  47.3 14.9 %collective-permute-start.8 = (f32[512,128]{1,0:T(8,128)S(1)}, f32[512,128]{1,0:T(8,128)S(1)}, u32[]{:S(2)}, u32[]{:S(2)}) collective-permute-start(f32[512,128]{1,0:T(8,128)S(1)} %get-tuple-element.47), channel_id=1, source_target_pairs={{0,32},{32,64},{64,96},{96,128},{128,160},{160,192},{192,224},{224... | collective-permute-start | bytes 786440 | tf_op jit(solution)/shard_map/ppermute | solution.py:432
  48.2 14.0 %collective-permute-start.9 = (f32[512,128]{1,0:T(8,128)S(1)}, f32[512,128]{1,0:T(8,128)S(1)}, u32[]{:S(2)}, u32[]{:S(2)}) collective-permute-start(f32[512,128]{1,0:T(8,128)S(1)} %get-tuple-element.48.loca), channel_id=1, source_target_pairs={{0,224},{32,0},{64,32},{96,64},{128,96},{160,128},{192,160},{224,1... | collective-permute-start | bytes 786440 | tf_op jit(solution)/shard_map/ppermute | solution.py:432
  50.0 9.1 %collective-permute-start.10 = (f32[2,128]{1,0:T(2,128)S(1)}, f32[2,128]{1,0:T(2,128)S(1)}, u32[]{:S(2)}, u32[]{:S(2)}) collective-permute-start(f32[2,128]{1,0:T(2,128)S(1)} %get-tuple-element.50), channel_id=1, source_target_pairs={{0,4},{4,8},{8,12},{12,16},{16,20},{20,24},{24,28},{28,0},{1,5},{5... | collective-permute-start | bytes 3080 | tf_op jit(solution)/shard_map/ppermute | solution.py:432
  56.2 5.9 %collective-permute-start.12 = (f32[2,1024]{1,0:T(2,128)S(1)}, f32[2,1024]{1,0:T(2,128)S(1)}, u32[]{:S(2)}, u32[]{:S(2)}) collective-permute-start(f32[2,1024]{1,0:T(2,128)S(1)} %get-tuple-element.52), channel_id=1, source_target_pairs={{0,1},{1,2},{2,3},{3,0},{4,5},{5,6},{6,7},{7,4},{8,9},{9,10},{10,1... | collective-permute-start | bytes 24584 | tf_op jit(solution)/shard_map/ppermute | solution.py:432
  57.6 4.6 %collective-permute-start.13 = (f32[2,1024]{1,0:T(2,128)S(1)}, f32[2,1024]{1,0:T(2,128)S(1)}, u32[]{:S(2)}, u32[]{:S(2)}) collective-permute-start(f32[2,1024]{1,0:T(2,128)S(1)} %get-tuple-element.53), channel_id=1, source_target_pairs={{0,3},{1,0},{2,1},{3,2},{4,7},{5,4},{6,5},{7,6},{8,11},{9,8},{10,9... | collective-permute-start | bytes 24584 | tf_op jit(solution)/shard_map/ppermute | solution.py:432
  59.2 3.0 %collective-permute-start.11 = (f32[2,128]{1,0:T(2,128)S(1)}, f32[2,128]{1,0:T(2,128)S(1)}, u32[]{:S(2)}, u32[]{:S(2)}) collective-permute-start(f32[2,128]{1,0:T(2,128)S(1)} %get-tuple-element.51), channel_id=1, source_target_pairs={{0,28},{4,0},{8,4},{12,8},{16,12},{20,16},{24,20},{28,24},{1,29},{... | collective-permute-start | bytes 3080 | tf_op jit(solution)/shard_map/ppermute | solution.py:432

commit v2 on v1

--- a/solution.py
+++ b/solution.py
@@ -64,63 +64,29 @@
     return jnp.broadcast_to(gates[:, index : index + 1], like).astype(BF16)
 
 
-def forward_kernel(
-    rhs_hbm, linv_hbm, loff_hbm, uinv_hbm, uoff_hbm, coupling_hbm, sep_hbm, from_hbm,
-    m_ref, p_ref, t_ref, gates_ref, mats_ref,
-    rhs, linv, loff, uinv, uoff, coupling, sep, link, sems,
-):
-    planes = rhs.shape[0]
+def block(ref, first, count, size=128):
+    return ref[0, first * size : (first + count) * size, :], ref[1, first * size : (first + count) * size, :]
+
+
+def keep(ref, index, value):
+    size = value[0].shape[0]
+    for part in range(2):
+        ref[part, index * size : (index + 1) * size, :] = value[part]
+
+
+def fetcher(sems):
     copies = {}
 
     def fetch(name, source, target):
         copies[name] = pltpu.make_async_copy(source, target, sems.at[len(copies)])
         copies[name].start()
 
-    fetch("coupling", coupling_hbm.at[0], coupling)
-    fetch("linv", linv_hbm.at[:, 0, 0], linv)
-    fetch(0, rhs_hbm.at[0], rhs.at[0])
-    fetch("loff", loff_hbm.at[:, 0, 0], loff)
-    fetch("uinv", uinv_hbm.at[:, 0, 0], uinv)
-    fetch("uoff", uoff_hbm.at[:, 0, 0], uoff)
-    for plane in range(1, planes):
-        fetch(plane, rhs_hbm.at[plane], rhs.at[plane])
-    fetch("sep", sep_hbm.at[0], sep)
-    fetch("link", from_hbm, link)
-
-    copies["coupling"].wait()
-    gate_rows = coupling[...].astype(F32)
-    rows = [gate_rows[p : p + 1] for p in range(planes - 1)]
-    prefix = [jnp.ones_like(rows[0])]
-    for row in rows:
-        prefix.append(prefix[-1] * row)
-    open_any = [jnp.max(row, axis=1, keepdims=True) for row in prefix]
-    gates = jnp.transpose(jnp.concatenate(rows + [jnp.zeros_like(rows[0])] + prefix, axis=0))
-    gates_ref[...] = gates
+    return copies, fetch
+
+
+def forward_rows(copies, rhs, t_ref, gates, lower_ref, back_ref, upper_ref, link, sep, m_ref, p_ref):
+    planes = rhs.shape[0]
     like = rhs.shape[1:]
-
-    for name in ("linv", "loff", "uinv", "uoff"):
-        copies[name].wait()
-    lower = [halves(linv[p]) for p in range(planes)]
-    upper = [halves(uinv[p]) for p in range(planes)]
-    links_l, links_u = [None], []
-    for p in range(1, planes):
-        merged = product(halves(loff[p - 1]), lower[p])
-        mats_ref[p - 1] = merged
-        links_l.append(halves(merged))
-    for p in range(planes - 1):
-        merged = product(halves(uoff[p]), upper[p])
-        mats_ref[planes - 1 + p] = merged
-        links_u.append(halves(merged))
-    back = [upper[0]]
-    mats_ref[2 * planes - 2] = uinv[0]
-    tail = None
-    for p in range(1, planes):
-        step = (-open_any[p]) * mats_ref[planes - 1 + p - 1]
-        tail = step if tail is None else small(step, tail)
-        full = product(upper[p], halves(tail))
-        mats_ref[2 * planes - 2 + p] = full
-        back.append(halves(full))
-
     total = None
     pending = None
     previous = None
@@ -128,67 +94,126 @@
         copies[p].wait()
         source = halves(rhs[p])
         if p == 0:
-            running = product(source, lower[0])
+            running = product(source, block(lower_ref, 0, 1))
         else:
             gated = masked(previous, -column(gates, p - 1, like))
-            running = product(side(source, gated), over(lower[p], links_l[p]))
+            running = product(side(source, gated), block(lower_ref, 2 * p - 1, 2))
         t_ref[p] = running
         previous = halves(running)
         part = previous if p == 0 else masked(previous, column(gates, planes + p, like))
         if p % 2 == 0:
             pending = part
         else:
-            term = product(side(pending, part), over(back[p - 1], back[p]))
+            term = product(side(pending, part), block(back_ref, p - 1, 2))
             total = term if total is None else total + term
     copies["link"].wait()
-    m_ref[...] = link[1] * product(previous, upper[planes - 1])
+    m_ref[...] = link[1] * product(previous, block(upper_ref, 2 * planes - 2, 1))
     copies["sep"].wait()
     p_ref[...] = sep[...] + link[0] * total
 
 
-def backward_kernel(t_ref, gates_ref, mats_ref, linv_ref, uinv_ref, x_ref, apply_ref, sweep_ref, mask_ref):
-    planes = t_ref.shape[0]
+def forward_kernel(
+    rhs_hbm, linv_hbm, loff_hbm, uinv_hbm, uoff_hbm, coupling_hbm, sep_hbm, from_hbm,
+    m_ref, p_ref, t_ref, gates_ref, lower_ref, upper_ref, back_ref,
+    rhs, linv, loff, uinv, uoff, coupling, sep, link, sems,
+):
+    planes, count, _ = rhs.shape
+    copies, fetch = fetcher(sems)
+    fetch("coupling", coupling_hbm, coupling)
+    fetch("linv", linv_hbm.at[:, 0, 0], linv)
+    fetch("loff", loff_hbm.at[:, 0, 0], loff)
+    fetch("uinv", uinv_hbm.at[:, 0, 0], uinv)
+    fetch("uoff", uoff_hbm.at[:, 0, 0], uoff)
+    for plane in range(planes):
+        fetch(plane, rhs_hbm.at[plane, :count], rhs.at[plane])
+    fetch("link", from_hbm.at[:, :count], link)
+    fetch("sep", sep_hbm.at[0, :count], sep)
+
+    copies["coupling"].wait()
+    tiles = coupling[...].astype(F32)
+    rows = [
+        jnp.concatenate([tiles[p, q : q + 1] for q in range(tiles.shape[1])], axis=1) for p in range(planes - 1)
+    ]
+    prefix = [jnp.ones_like(rows[0])]
+    for row in rows:
+        prefix.append(prefix[-1] * row)
+    open_any = [jnp.max(row, axis=1, keepdims=True) for row in prefix]
+    gates = jnp.transpose(jnp.concatenate(rows + [jnp.zeros_like(rows[0])] + prefix, axis=0))
+    gates_ref[...] = gates
+
+    for name in ("linv", "loff", "uinv", "uoff"):
+        copies[name].wait()
+    lower = [halves(linv[p]) for p in range(planes)]
+    upper = [halves(uinv[p]) for p in range(planes)]
+    keep(lower_ref, 0, lower[0])
+    for p in range(1, planes):
+        keep(lower_ref, 2 * p - 1, lower[p])
+        keep(lower_ref, 2 * p, halves(product(halves(loff[p - 1]), lower[p])))
+    merged = []
+    for p in range(planes):
+        keep(upper_ref, 2 * p, upper[p])
+        if p < planes - 1:
+            merged.append(product(halves(uoff[p]), upper[p]))
+            keep(upper_ref, 2 * p + 1, halves(merged[p]))
+    keep(back_ref, 0, upper[0])
+    tail = None
+    for p in range(1, planes):
+        step = (-open_any[p]) * merged[p - 1]
+        tail = halves(step if tail is None else product(halves(step), tail))
+        keep(back_ref, p, halves(product(upper[p], tail)))
+    forward_rows(copies, rhs, t_ref, gates[:count], lower_ref, back_ref, upper_ref, link, sep, m_ref, p_ref)
+
+
+def forward_rest_kernel(
+    rhs_hbm, sep_hbm, from_hbm, gates_ref, lower_ref, upper_ref, back_ref,
+    m_ref, p_ref, t_ref,
+    rhs, sep, link, sems,
+):
+    planes, count, _ = rhs.shape
+    copies, fetch = fetcher(sems)
+    for plane in range(planes):
+        fetch(plane, rhs_hbm.at[plane, count:], rhs.at[plane])
+    fetch("link", from_hbm.at[:, count:], link)
+    fetch("sep", sep_hbm.at[0, count:], sep)
+    forward_rows(copies, rhs, t_ref, gates_ref[count:], lower_ref, back_ref, upper_ref, link, sep, m_ref, p_ref)
+
+
+def backward_kernel(
+    ta_ref, tb_ref, gates_ref, lower_ref, upper_ref, back_ref, x_ref, apply_ref, sweep_ref, mask_ref
+):
+    planes, _, width = ta_ref.shape
     gates = gates_ref[...]
-    like = t_ref.shape[1:]
-    upper = [halves(uinv_ref[p, 0, 0]) for p in range(planes)]
-    links_u = [halves(mats_ref[planes - 1 + p]) for p in range(planes - 1)]
-    size = like[1]
-
-    def keep(ref, index, value):
-        for part in range(2):
-            ref[part, index * size : (index + 1) * size, :] = value[part]
+    like = (gates.shape[0], width)
+    one = lambda ref, index: block(ref, index, 1)
 
     open_any = [jnp.max(gates[:, planes + p : planes + p + 1], axis=0, keepdims=True) for p in range(planes)]
-    first = halves(linv_ref[0, 0, 0])
-    last = halves(linv_ref[planes - 1, 0, 0])
-    running = linv_ref[0, 0, 0]
+    now = one(lower_ref, 0)
+    last = one(lower_ref, 2 * planes - 3)
     for p in range(planes):
         if p > 0:
-            running = product(halves(running), halves((-open_any[p]) * mats_ref[p - 1]))
-        now = halves(running) if p > 0 else first
-        full = halves(mats_ref[2 * planes - 2 + p])
+            now = halves((-open_any[p]) * product(now, one(lower_ref, 2 * p)))
+        full = one(back_ref, p)
         keep(apply_ref, p, halves(product(now, full)))
         if p < planes - 1:
-            keep(sweep_ref, 2 * p, halves(product(now, upper[p])))
-            keep(sweep_ref, 2 * p + 1, links_u[p])
+            keep(sweep_ref, 2 * p, halves(product(now, one(upper_ref, 2 * p))))
+            keep(sweep_ref, 2 * p + 1, one(upper_ref, 2 * p + 1))
         else:
             keep(apply_ref, planes, halves(product(last, full)))
-            keep(apply_ref, planes + 1, halves(product(last, upper[p])))
-            keep(apply_ref, planes + 2, halves(product(now, upper[p])))
-
-    solved = product(halves(t_ref[planes - 1]), upper[planes - 1])
+            keep(apply_ref, planes + 1, halves(product(last, one(upper_ref, 2 * p))))
+            keep(apply_ref, planes + 2, halves(product(now, one(upper_ref, 2 * p))))
+
+    def lowered(p):
+        return halves(jnp.concatenate([ta_ref[p], tb_ref[p]], axis=0))
+
+    solved = product(lowered(planes - 1), one(upper_ref, 2 * planes - 2))
     x_ref[planes - 1] = solved
     for p in range(planes - 2, -1, -1):
         mask = -column(gates, p, like)
         mask_ref[p] = mask
-        solved = product(side(halves(t_ref[p]), masked(halves(solved), mask)), over(upper[p], links_u[p]))
+        solved = product(side(lowered(p), masked(halves(solved), mask)), block(upper_ref, 2 * p, 2))
         x_ref[p] = solved
     for p in range(1, planes):
         mask_ref[planes - 2 + p] = column(gates, planes + p, like)
-
-
-def block(ref, first, count, size=128):
-    return ref[0, first * size : (first + count) * size, :], ref[1, first * size : (first + count) * size, :]
 
 
 def slab(vector, following, into_ref, mask_ref, apply_ref):
@@ -250,12 +275,14 @@
 
 
 def first_kernel(
-    p_ref, m_ref, m_prev, p_next, into_ref, from_ref, diag_ref, mask_ref, apply_ref,
+    pa, pb, ma, mb, ma_prev, mb_prev, pa_next, pb_next, into_ref, from_ref, diag_ref, mask_ref, apply_ref,
     k_ref, kn_ref, mm_ref, loc_ref, row_first, row_last, column_first, column_last,
 ):
     flags = neighbours()
-    vector = p_ref[...] + only(flags, BEFORE, m_prev[...])
-    following = only(flags, AFTER, p_next[...] + m_ref[...])
+    own = (pa[...] + only(flags, BEFORE, ma_prev[...]), pb[...] + only(flags, BEFORE, mb_prev[...]))
+    other = (only(flags, AFTER, pa_next[...] + ma[...]), only(flags, AFTER, pb_next[...] + mb[...]))
+    vector = jnp.concatenate(own, axis=0)
+    following = jnp.concatenate(other, axis=0)
     k_ref[...] = vector
     kn_ref[...] = following
     put_rims((vector, following), (row_first, row_last, column_first, column_last))
@@ -266,7 +293,7 @@
 
 def second_kernel(
     loc_ref, mm_ref, mm_prev, loc_next, row_low, row_high, column_low, column_high,
-    into_ref, from_ref, diag_ref, mask_ref, apply_ref,
+    into_ref, from_ref, diag_ref, mask_ref, apply_ref, x0_ref,
     k_ref, kn_ref, mma_ref, mmb_ref, loca_ref, locb_ref, row_first, row_last, column_first, column_last,
 ):
     flags = neighbours()
@@ -441,54 +468,78 @@
 
     rim_shapes = [shape(2, width), shape(2, width), shape(2, count), shape(2, count)]
 
-    m, p, t, gates, mats = call(
+    def in_hbm(*arrays):
+        return [pltpu.with_memory_space_constraint(array, pltpu.HBM) for array in arrays]
+
+    part = shape(half, width)
+    tall = shape(planes, half, width)
+
+    def stack(number):
+        return shape(2, number * width, width, dtype=BF16)
+
+    staged = [
+        pltpu.VMEM((half, width), F32),
+        pltpu.VMEM((2, half, width), F32),
+        pltpu.SemaphoreType.DMA((planes + 7,)),
+    ]
+    ma, pa, ta, gates, lower, upper, back = call(
         forward_kernel,
         "forward",
         outside(8, pltpu.HBM),
-        [plane, plane, shape(planes, count, width), shape(count, 2 * planes), shape(3 * planes - 2, width, width)],
-        inside(5),
+        [part, part, tall, shape(count, 2 * planes), stack(2 * planes - 1), stack(2 * planes - 1), stack(planes)],
+        inside(7),
         [
-            pltpu.VMEM((planes, count, width), F32),
+            pltpu.VMEM((planes, half, width), F32),
             pltpu.VMEM((planes, width, width), F32),
             pltpu.VMEM((planes - 1, width, width), F32),
             pltpu.VMEM((planes, width, width), F32),
             pltpu.VMEM((planes - 1, width, width), F32),
-            pltpu.VMEM((planes - 1, count), jnp.int32),
-            pltpu.VMEM((count, width), F32),
-            pltpu.VMEM((2, count, width), F32),
-            pltpu.SemaphoreType.DMA((planes + 7,)),
+            pltpu.VMEM((planes - 1, count // width, width), jnp.int32),
+            *staged,
         ],
-        flops=dense * 24,
-        moved=12 << 20,
-    )(*(
-        pltpu.with_memory_space_constraint(array, pltpu.HBM)
-        for array in (rhs_interior, lower_inv, lower_off, upper_inv, upper_off, coupling, rhs_sep, link_from)
-    ))
-    m_prev = along(m, "gx", 1)
-    p_next = along(p, "gx", -1)
+        flops=dense * 16,
+        moved=8 << 20,
+    )(
+        *in_hbm(rhs_interior, lower_inv, lower_off, upper_inv, upper_off),
+        *in_hbm(coupling.reshape(planes - 1, count // width, width), rhs_sep, link_from),
+    )
+    ma_prev = along(ma, "gx", 1)
+    pa_next = along(pa, "gx", -1)
+    mb, pb, tb = call(
+        forward_rest_kernel,
+        "forward_rest",
+        outside(3, pltpu.HBM) + inside(4),
+        [part, part, tall],
+        inside(3),
+        [pltpu.VMEM((planes, half, width), F32), *staged],
+        flops=dense * 12,
+        moved=4 << 20,
+    )(*in_hbm(rhs_interior, rhs_sep, link_from), gates, lower, upper, back)
+    mb_prev = along(mb, "gx", 1)
+    pb_next = along(pb, "gx", -1)
     x, applied, swept, masks = call(
         backward_kernel,
         "backward",
-        inside(5),
+        inside(6),
         [
             shape(planes, count, width),
-            shape(2, (planes + 3) * width, width, dtype=BF16),
-            shape(2, (2 * planes - 2) * width, width, dtype=BF16),
+            stack(planes + 3),
+            stack(2 * planes - 2),
             shape(2 * planes - 2, count, width, dtype=BF16),
         ],
         inside(4),
         flops=dense * 20,
         moved=12 << 20,
-    )(t, gates, mats, lower_inv, upper_inv)
+    )(ta, tb, gates, lower, upper, back)
     k0, k0n, mm, loc, *edges = call(
         first_kernel,
         "first",
-        inside(9),
+        inside(13),
         [plane] * 4 + rim_shapes,
         inside(8),
         flops=dense * 11,
         moved=4 << 20,
-    )(p, m, m_prev, p_next, link_into, link_from, sep_diag, masks, applied)
+    )(pa, pb, ma, mb, ma_prev, mb_prev, pa_next, pb_next, link_into, link_from, sep_diag, masks, applied)
     mm_prev = along(mm, "gx", 1)
     loc_next = along(loc, "gx", -1)
     arrived = rims(*edges)
@@ -505,16 +556,15 @@
         )(k, kn, link_into, masks, applied, swept)
 
     x0 = swept_field("sweep_first", k0, k0n)
-    part = shape(half, width)
     k1, k1n, mma, mmb, loca, locb, *edges = call(
         second_kernel,
         "second",
-        inside(13),
+        inside(13) + outside(1),
         [plane] * 2 + [part] * 4 + rim_shapes,
         inside(10),
         flops=dense * 11,
         moved=4 << 20,
-    )(loc, mm, mm_prev, loc_next, *arrived, link_into, link_from, sep_diag, masks, applied)
+    )(loc, mm, mm_prev, loc_next, *arrived, link_into, link_from, sep_diag, masks, applied, x0)
     mmb_prev = along(mmb, "gx", 1)
     loca_next = along(loca, "gx", -1)
     arrived = rims(*edges)

time: 88.2 us -> 86 us (0.975)
  waiting for transfers between devices: 10.2 us -> 4.56 us
  Pallas kernels: 25.8 us -> 28.4 us
  starting transfers between devices: 27.6 us -> 29.6 us
  local copies, waits for them, and re-layouts: 1.49 us -> 0.02 us
    ppermute x14 -> x16, waiting for transfers between devices: 10.2 us -> 4.56 us  [along(): lax.ppermute(value, axis, [(i, (i + by) % size) for i in range(size)])]
    pallas_call x4 -> x5, Pallas kernels: 17.5 us -> 20.1 us  [the longest x1 6.92 us: body(): call(forward_kernel, 'forward', outside(8, pltpu.HBM), [part, part, tall,...]
    ppermute x14 -> x16, starting transfers between devices: 27.6 us -> 29.6 us  [along(): lax.ppermute(value, axis, [(i, (i + by) % size) for i in range(size)])]
    unnamed x11 -> x6, local copies, waits for them, and re-layouts: 1.49 us -> 0.02 us
  transfers between devices with their start and end apart: 14 -> 16, of which waited for: 4 -> 3; matrix products, arithmetic and copies ran while one was open for 0% -> 0% of each run, Pallas kernels for 10% -> 16%
where the time goes in v2:
time: 86 us; the launch traced here: 85.8 us
  starting transfers between devices  29.6 us (34%)
  Pallas kernels  28.4 us (33%)
  blocking collectives  22.2 us (26%)
  waiting for transfers between devices  4.56 us (5%)
  between operations  1.02 us (1%)
    ppermute x16, starting transfers between devices, along(): lax.ppermute(value, axis, [(i, (i + by) % size) for i in range(size)])  29.6 us
    all_to_all x1, blocking collectives, body(): gathered = lax.all_to_all(line, AXES, 0, 0, tiled=True)  22.2 us
    pallas_call x1, Pallas kernels, body(): call(forward_kernel, 'forward', outside(8, pltpu.HBM), [part, part, tall,...  6.92 us
    pallas_call x2, Pallas kernels, swept_field(): call(sweep_kernel, name, inside(6), shape(planes, count, width), pl.Block...  4.72 us
    pallas_call x1, Pallas kernels, body(): call(forward_rest_kernel, 'forward_rest', outside(3, pltpu.HBM) + inside(...  4.68 us
    ppermute x16, waiting for transfers between devices, along(): lax.ppermute(value, axis, [(i, (i + by) % size) for i in range(size)])  4.56 us
    pallas_call x1, Pallas kernels, body(): call(backward_kernel, 'backward', inside(6), [shape(planes, count, width)...  3.96 us
    pallas_call x1, Pallas kernels, body(): call(second_kernel, 'second', inside(13) + outside(1), [plane] * 2 + [par...  2.7 us
  transfers between devices with their start and end apart: 16, of which 3 were waited for; matrix products, arithmetic and copies ran while one was open for 0% of the time, Pallas kernels for 16%

profile of v2, /device:TPU:1, one launch (start us, length us, event | category | flops | bytes accessed | tf_op | source)
XLA Modules:
  0.0 85.8 jit_solution(17670011429133200245)
XLA Ops:
  0.6 6.9 %forward.1 = (f32[512,128]{1,0:T(8,128)S(1)}, f32[512,128]{1,0:T(8,128)S(1)}, f32[8,512,128]{2,1,0:T(8,128)S(1)}, f32[1024,16]{1,0:T(8,128)S(1)}, bf16[2,1920,12...) custom-call(f32[8,1024,128]{2,1,0:T(8,128)} %rhs_hbm.3, ...), custom_call_target="tpu_custom_call" | custom-call | flops 1073741824 | bytes 8388608 | tf_op jit(solution)/shard_map/forward/pallas_call | solution.py:485
  7.6 6.5 %collective-permute-start.2 = (f32[512,128]{1,0:T(8,128)S(1)}, f32[512,128]{1,0:T(8,128)S(1)}, u32[]{:S(2)}, u32[]{:S(2)}) collective-permute-start(f32[512,128]{1,0:T(8,128)S(1)} %get-tuple-element.34.pa), channel_id=1, source_target_pairs={{0,224},{32,0},{64,32},{96,64},{128,96},{160,128},{192,160},{224,1... | collective-permute-start | bytes 786440 | tf_op jit(solution)/shard_map/ppermute | solution.py:459
  14.0 0.0 collective-permute-start
  14.1 4.7 %forward_rest.1 = (f32[512,128]{1,0:T(8,128)S(1)}, f32[512,128]{1,0:T(8,128)S(1)}, f32[8,512,128]{2,1,0:T(8,128)S(1)}) custom-call(f32[8,1024,128]{2,1,0:T(8,128)} %rhs_hbm.3, f32[1,1024,128]{2,1,0:T(8,128)} %sep_hbm.3, f32[2,1024,128]{2,1,0:T(8,128)} %from_ref.3, f32[1024,16]{1,0:T(8,128)S(1)} %get-tuple-element.35.gates_ref, ...), custom_call_target="tpu_custom_call" | custom-call | flops 805306368 | bytes 4194304 | tf_op jit(solution)/shard_map/forward_rest/pallas_call | solution.py:508
  18.7 0.0 copy-start
  18.7 0.0 copy-start.1
  18.8 0.0 copy-start.2
  18.8 2.7 %collective-permute-start.3 = (f32[512,128]{1,0:T(8,128)S(1)}, f32[512,128]{1,0:T(8,128)S(1)}, u32[]{:S(2)}, u32[]{:S(2)}) collective-permute-start(f32[512,128]{1,0:T(8,128)S(1)} %get-tuple-element.39.pb), channel_id=1, source_target_pairs={{0,224},{32,0},{64,32},{96,64},{128,96},{160,128},{192,160},{224,1... | collective-permute-start | bytes 786440 | tf_op jit(solution)/shard_map/ppermute | solution.py:459
  21.5 0.0 collective-permute-start.1
  21.5 4.0 %backward.1 = (f32[8,1024,128]{2,1,0:T(8,128)S(1)}, bf16[2,1408,128]{2,1,0:T(8,128)(2,1)S(1)}, bf16[2,1792,128]{2,1,0:T(8,128)(2,1)S(1)}, bf16[14,1024,128]{2,1,0:T(8,128)(2,1)S(1)}) custom-call(f32[8,512,128]{2,1,0:T(8,128)S(1)} %get-tuple-element.42.ta_ref, f32[8,512,128]{2,1,0:T(8,128)S(1)} %get-tuple-element.43.tb_ref, ...), custom_call_target="tpu_custom_call" | custom-call | flops 1342177280 | bytes 12582912 | tf_op jit(solution)/shard_map/backward/pallas_call | solution.py:520
  25.5 0.0 collective-permute-done.2.pa_next
  25.5 0.0 collective-permute-done.ma_prev
  25.5 0.4 collective-permute-done.3.pb_next
  25.9 3.1 %collective-permute-done.1.mb_prev = f32[512,128]{1,0:T(8,128)S(1)} collective-permute-done((f32[512,128]{1,0:T(8,128)S(1)}, f32[512,128]{1,0:T(8,128)S(1)}, u32[]{:S(2)}, u32[]{:S(2)}) %collective-permute-start.1) | collective-permute-done | bytes 262176 | tf_op jit(solution)/shard_map/ppermute | solution.py:459
  29.0 0.0 copy-done
  29.0 0.0 copy-done.1
  29.0 0.0 copy-done.2
  29.0 1.8 %first.1 = (f32[1024,128]{1,0:T(8,128)S(1)}, f32[1024,128]{1,0:T(8,128)S(1)}, f32[1024,128]{1,0:T(8,128)S(1)}, f32[1024,128]{1,0:T(8,128)S(1)}, f32[2,128]{1,0:T...) custom-call(f32[512,128]{1,0:T(8,128)S(1)} %get-tuple-element.34.pa, ...), custom_call_target="tpu_custom_call" | custom-call | flops 738197504 | bytes 4194304 | tf_op jit(solution)/shard_map/first/pallas_call | solution.py:534
  30.9 0.4 collective-permute-start.5
  31.2 1.2 %collective-permute-start.4 = (f32[1024,128]{1,0:T(8,128)S(1)}, f32[1024,128]{1,0:T(8,128)S(1)}, u32[]{:S(2)}, u32[]{:S(2)}) collective-permute-start(f32[1024,128]{1,0:T(8,128)S(1)} %get-tuple-element.49.mm_ref), channel_id=1, source_target_pairs={{0,32},{32,64},{64,96},{96,128},{128,160},{160,192},{192,224},{224... | collective-permute-start | bytes 1572872 | tf_op jit(solution)/shard_map/ppermute | solution.py:459
  32.4 4.1 %collective-permute-start.6 = (f32[2,128]{1,0:T(2,128)S(1)}, f32[2,128]{1,0:T(2,128)S(1)}, u32[]{:S(2)}, u32[]{:S(2)}) collective-permute-start(f32[2,128]{1,0:T(2,128)S(1)} %get-tuple-element.50), channel_id=1, source_target_pairs={{0,4},{4,8},{8,12},{12,16},{16,20},{20,24},{24,28},{28,0},{1,5},{5... | collective-permute-start | bytes 3080 | tf_op jit(solution)/shard_map/ppermute | solution.py:459
  36.5 0.0 collective-permute-start.7
  36.5 1.3 %collective-permute-start.8 = (f32[2,1024]{1,0:T(2,128)S(1)}, f32[2,1024]{1,0:T(2,128)S(1)}, u32[]{:S(2)}, u32[]{:S(2)}) collective-permute-start(f32[2,1024]{1,0:T(2,128)S(1)} %get-tuple-element.52), channel_id=1, source_target_pairs={{0,1},{1,2},{2,3},{3,0},{4,5},{5,6},{6,7},{7,4},{8,9},{9,10},{10,1... | collective-permute-start | bytes 24584 | tf_op jit(solution)/shard_map/ppermute | solution.py:459
  37.8 0.0 collective-permute-done.6.row_low
  37.8 2.2 %collective-permute-start.9 = (f32[2,1024]{1,0:T(2,128)S(1)}, f32[2,1024]{1,0:T(2,128)S(1)}, u32[]{:S(2)}, u32[]{:S(2)}) collective-permute-start(f32[2,1024]{1,0:T(2,128)S(1)} %get-tuple-element.53), channel_id=1, source_target_pairs={{0,3},{1,0},{2,1},{3,2},{4,7},{5,4},{6,5},{7,6},{8,11},{9,8},{10,9... | collective-permute-start | bytes 24584 | tf_op jit(solution)/shard_map/ppermute | solution.py:459
  40.0 2.4 %sweep_first.1.x0_ref = f32[8,1024,128]{2,1,0:T(8,128)S(1)} custom-call(f32[1024,128]{1,0:T(8,128)S(1)} %get-tuple-element.46.k.k0, f32[1024,128]{1,0:T(8,128)S(1)} %get-tuple-element.47.kn.k0n, f32[2,1024,128]{2,1,0:T(8,128)S(1)} %copy-done.1, bf16[14,1024,128]{2,1,0:T(8,128)(2,1)S(1)} %get-tuple-element.44.mask_ref, ...), custom_call_target="tpu_custom_call" | custom-call | flops 1073741824 | bytes 8388608 | tf_op jit(solution)/shard_map/sweep_first/pallas_call | solution.py:548
  42.3 0.0 collective-permute-done.7.row_high
  42.4 0.0 collective-permute-done.8.column_low
  42.4 0.0 collective-permute-done.9.column_high
  42.4 0.0 collective-permute-done.5.loc_next
  42.4 1.0 %collective-permute-done.4.mm_prev = f32[1024,128]{1,0:T(8,128)S(1)} collective-permute-done((f32[1024,128]{1,0:T(8,128)S(1)}, f32[1024,128]{1,0:T(8,128)S(1)}, u32[]{:S(2)}, u32[]{:S(2)}) %collective-permute-start.4) | collective-permute-done | bytes 524320 | tf_op jit(solution)/shard_map/ppermute | solution.py:459
  43.4 2.7 %second.1 = (f32[1024,128]{1,0:T(8,128)S(1)}, f32[1024,128]{1,0:T(8,128)S(1)}, f32[512,128]{1,0:T(8,128)S(1)}, f32[512,128]{1,0:T(8,128)S(1)}, f32[512,128]{1,0:...) custom-call(f32[1024,128]{1,0:T(8,128)S(1)} %get-tuple-element.48.lo, ...), custom_call_target="tpu_custom_call" | custom-call | flops 738197504 | bytes 4194304 | tf_op jit(solution)/shard_map/second/pallas_call | solution.py:559
  46.1 0.1 collective-permute-start.10
  46.2 2.7 %collective-permute-start.11 = (f32[512,128]{1,0:T(8,128)S(1)}, f32[512,128]{1,0:T(8,128)S(1)}, u32[]{:S(2)}, u32[]{:S(2)}) collective-permute-start(f32[512,128]{1,0:T(8,128)S(1)} %get-tuple-element.59.loca), channel_id=1, source_target_pairs={{0,224},{32,0},{64,32},{96,64},{128,96},{160,128},{192,160},{224,1... | collective-permute-start | bytes 786440 | tf_op jit(solution)/shard_map/ppermute | solution.py:459
  48.9 5.0 %collective-permute-start.12 = (f32[2,128]{1,0:T(2,128)S(1)}, f32[2,128]{1,0:T(2,128)S(1)}, u32[]{:S(2)}, u32[]{:S(2)}) collective-permute-start(f32[2,128]{1,0:T(2,128)S(1)} %get-tuple-element.61), channel_id=1, source_target_pairs={{0,4},{4,8},{8,12},{12,16},{16,20},{20,24},{24,28},{28,0},{1,5},{5... | collective-permute-start | bytes 3080 | tf_op jit(solution)/shard_map/ppermute | solution.py:459
  53.9 0.0 collective-permute-start.13
  53.9 1.3 %collective-permute-start.14 = (f32[2,1024]{1,0:T(2,128)S(1)}, f32[2,1024]{1,0:T(2,128)S(1)}, u32[]{:S(2)}, u32[]{:S(2)}) collective-permute-start(f32[2,1024]{1,0:T(2,128)S(1)} %get-tuple-element.63), channel_id=1, source_target_pairs={{0,1},{1,2},{2,3},{3,0},{4,5},{5,6},{6,7},{7,4},{8,9},{9,10},{10,1... | collective-permute-start | bytes 24584 | tf_op jit(solution)/shard_map/ppermute | solution.py:459
  55.2 0.0 collective-permute-done.12.row_low
  55.2 2.2 %collective-permute-start.15 = (f32[2,1024]{1,0:T(2,128)S(1)}, f32[2,1024]{1,0:T(2,128)S(1)}, u32[]{:S(2)}, u32[]{:S(2)}) collective-permute-start(f32[2,1024]{1,0:T(2,128)S(1)} %get-tuple-element.64), channel_id=1, source_target_pairs={{0,3},{1,0},{2,1},{3,2},{4,7},{5,4},{6,5},{7,6},{8,11},{9,8},{10,9... | collective-permute-start | bytes 24584 | tf_op jit(solution)/shard_map/ppermute | solution.py:459
  57.4 2.4 %sweep_second.1.x1_ref = f32[8,1024,128]{2,1,0:T(8,128)S(1)} custom-call(f32[1024,128]{1,0:T(8,128)S(1)} %get-tuple-element.55.k.k1, f32[1024,128]{1,0:T(8,128)S(1)} %get-tuple-element.56.kn.k1n, f32[2,1024,128]{2,1,0:T(8,128)S(1)} %copy-done.1, bf16[14,1024,128]{2,1,0:T(8,128)(2,1)S(1)} %get-tuple-element.44.mask_ref, ...), custom_call_target="tpu_custom_call" | custom-call | flops 1073741824 | bytes 8388608 | tf_op jit(solution)/shard_map/sweep_second/pallas_call | solution.py:548
  59.7 0.0 collective-permute-done.13.row_high
  59.7 0.0 collective-permute-done.14.column_low
  59.8 0.0 collective-permute-done.15.column_high
  59.8 0.0 collective-permute-done.10.mmb_prev
  59.8 0.0 collective-permute-done.11.loca_next
  59.8 1.0 %sums.1 = f32[256,128]{1,0:T(8,128)S(1)} custom-call(f32[1024,128]{1,0:T(8,128)S(1)} %get-tuple-element.46.k.k0, f32[1024,128]{1,0:T(8,128)S(1)} %get-tuple-element.47.kn.k0n, f32[1024,128]{1,0:T(8,128)S(1)} %get-tuple-element.55.k.k1, f32[1024,128]{1,0:T(8,128)S(1)} %get-tuple-element.56.kn.k1n, f32[512,128]{1,0:T(8,128)S(1)} %get-tuple-element.57.mma, ...), custom_call_target="tpu_custom_call" | custom-call | flops 67108864 | bytes 4194304 | tf_op jit(solution)/shard_map/sums/pallas_call | solution.py:572
  60.8 22.2 %all_to_all.11 = f32[256,1,128]{2,1,0:T(1,128)S(1)} all-to-all(f32[256,1,128]{2,1,0:T(1,128)S(1)} %bitcast.5), channel_id=1, replica_groups=mesh['gx'=8,'gy'=8,'gz'=4] {'gx','gy','gz'}, dimensions={0} | all-to-all | bytes 262144 | tf_op jit(solution)/shard_map/all_to_all | solution.py:581
  83.0 2.6 %final.1 = (f32[8,1024,128]{2,1,0:T(8,128)}, f32[1,1024,128]{2,1,0:T(8,128)}) custom-call(f32[256,128]{1,0:T(8,128)S(1)} %bitcast.6, f32[1024,128]{1,0:T(8,128)S(1)} %get-tuple-element.46.k.k0, f32[1024,128]{1,0:T(8,128)S(1)} %get-tuple-element.55.k.k1, f32[8,1024,128]{2,1,0:T(8,128)S(1)} %get-tuple-element.65.x_ref, f32[8,1024,128]{2,1,0:T(8,128)S(1)} %sweep_first.1.x0_ref, ...), custom_call_target="tpu_custom_call" | custom-call | flops 67108864 | bytes 16777216 | tf_op jit(solution)/shard_map/final/pallas_call | solution.py:582
Async XLA Ops:
  7.6 17.9 %collective-permute-start.2 = (f32[512,128]{1,0:T(8,128)S(1)}, f32[512,128]{1,0:T(8,128)S(1)}, u32[]{:S(2)}, u32[]{:S(2)}) collective-permute-start(f32[512,128]{1,0:T(8,128)S(1)} %get-tuple-element.34.pa), channel_id=1, source_target_pairs={{0,224},{32,0},{64,32},{96,64},{128,96},{160,128},{192,160},{224,1... | collective-permute-start | bytes 786440 | tf_op jit(solution)/shard_map/ppermute | solution.py:459
  14.0 11.5 %collective-permute-start = (f32[512,128]{1,0:T(8,128)S(1)}, f32[512,128]{1,0:T(8,128)S(1)}, u32[]{:S(2)}, u32[]{:S(2)}) collective-permute-start(f32[512,128]{1,0:T(8,128)S(1)} %get-tuple-element.40.ma), channel_id=1, source_target_pairs={{0,32},{32,64},{64,96},{96,128},{128,160},{160,192},{192,224},{224... | collective-permute-start | bytes 786440 | tf_op jit(solution)/shard_map/ppermute | solution.py:459
  18.7 10.3 %copy-start = (f32[2,1024,128]{2,1,0:T(8,128)S(1)}, f32[2,1024,128]{2,1,0:T(8,128)}, u32[]{:S(2)}) copy-start(f32[2,1024,128]{2,1,0:T(8,128)} %from_ref.3) | copy-start | bytes 3145732
  18.7 10.3 %copy-start.1 = (f32[2,1024,128]{2,1,0:T(8,128)S(1)}, f32[2,1024,128]{2,1,0:T(8,128)}, u32[]{:S(2)}) copy-start(f32[2,1024,128]{2,1,0:T(8,128)} %into_ref.7) | copy-start | bytes 3145732
  18.8 10.3 %copy-start.2 = (f32[1,1024,128]{2,1,0:T(8,128)S(1)}, f32[1,1024,128]{2,1,0:T(8,128)}, u32[]{:S(2)}) copy-start(f32[1,1024,128]{2,1,0:T(8,128)} %diag_ref.3) | copy-start | bytes 1572868
  18.8 7.1 %collective-permute-start.3 = (f32[512,128]{1,0:T(8,128)S(1)}, f32[512,128]{1,0:T(8,128)S(1)}, u32[]{:S(2)}, u32[]{:S(2)}) collective-permute-start(f32[512,128]{1,0:T(8,128)S(1)} %get-tuple-element.39.pb), channel_id=1, source_target_pairs={{0,224},{32,0},{64,32},{96,64},{128,96},{160,128},{192,160},{224,1... | collective-permute-start | bytes 786440 | tf_op jit(solution)/shard_map/ppermute | solution.py:459
  21.5 7.5 %collective-permute-start.1 = (f32[512,128]{1,0:T(8,128)S(1)}, f32[512,128]{1,0:T(8,128)S(1)}, u32[]{:S(2)}, u32[]{:S(2)}) collective-permute-start(f32[512,128]{1,0:T(8,128)S(1)} %get-tuple-element.41.mb), channel_id=1, source_target_pairs={{0,32},{32,64},{64,96},{96,128},{128,160},{160,192},{192,224},{224... | collective-permute-start | bytes 786440 | tf_op jit(solution)/shard_map/ppermute | solution.py:459
  30.9 11.5 %collective-permute-start.5 = (f32[1024,128]{1,0:T(8,128)S(1)}, f32[1024,128]{1,0:T(8,128)S(1)}, u32[]{:S(2)}, u32[]{:S(2)}) collective-permute-start(f32[1024,128]{1,0:T(8,128)S(1)} %get-tuple-element.48.loc_ref), channel_id=1, source_target_pairs={{0,224},{32,0},{64,32},{96,64},{128,96},{160,128},{192,160},{224,1... | collective-permute-start | bytes 1572872 | tf_op jit(solution)/shard_map/ppermute | solution.py:459
  31.2 12.2 %collective-permute-start.4 = (f32[1024,128]{1,0:T(8,128)S(1)}, f32[1024,128]{1,0:T(8,128)S(1)}, u32[]{:S(2)}, u32[]{:S(2)}) collective-permute-start(f32[1024,128]{1,0:T(8,128)S(1)} %get-tuple-element.49.mm_ref), channel_id=1, source_target_pairs={{0,32},{32,64},{64,96},{96,128},{128,160},{160,192},{192,224},{224... | collective-permute-start | bytes 1572872 | tf_op jit(solution)/shard_map/ppermute | solution.py:459
  32.4 5.4 %collective-permute-start.6 = (f32[2,128]{1,0:T(2,128)S(1)}, f32[2,128]{1,0:T(2,128)S(1)}, u32[]{:S(2)}, u32[]{:S(2)}) collective-permute-start(f32[2,128]{1,0:T(2,128)S(1)} %get-tuple-element.50), channel_id=1, source_target_pairs={{0,4},{4,8},{8,12},{12,16},{16,20},{20,24},{24,28},{28,0},{1,5},{5... | collective-permute-start | bytes 3080 | tf_op jit(solution)/shard_map/ppermute | solution.py:459
  36.5 5.8 %collective-permute-start.7 = (f32[2,128]{1,0:T(2,128)S(1)}, f32[2,128]{1,0:T(2,128)S(1)}, u32[]{:S(2)}, u32[]{:S(2)}) collective-permute-start(f32[2,128]{1,0:T(2,128)S(1)} %get-tuple-element.51), channel_id=1, source_target_pairs={{0,28},{4,0},{8,4},{12,8},{16,12},{20,16},{24,20},{28,24},{1,29},{... | collective-permute-start | bytes 3080 | tf_op jit(solution)/shard_map/ppermute | solution.py:459
  36.5 5.8 %collective-permute-start.8 = (f32[2,1024]{1,0:T(2,128)S(1)}, f32[2,1024]{1,0:T(2,128)S(1)}, u32[]{:S(2)}, u32[]{:S(2)}) collective-permute-start(f32[2,1024]{1,0:T(2,128)S(1)} %get-tuple-element.52), channel_id=1, source_target_pairs={{0,1},{1,2},{2,3},{3,0},{4,5},{5,6},{6,7},{7,4},{8,9},{9,10},{10,1... | collective-permute-start | bytes 24584 | tf_op jit(solution)/shard_map/ppermute | solution.py:459
  37.8 4.6 %collective-permute-start.9 = (f32[2,1024]{1,0:T(2,128)S(1)}, f32[2,1024]{1,0:T(2,128)S(1)}, u32[]{:S(2)}, u32[]{:S(2)}) collective-permute-start(f32[2,1024]{1,0:T(2,128)S(1)} %get-tuple-element.53), channel_id=1, source_target_pairs={{0,3},{1,0},{2,1},{3,2},{4,7},{5,4},{6,5},{7,6},{8,11},{9,8},{10,9... | collective-permute-start | bytes 24584 | tf_op jit(solution)/shard_map/ppermute | solution.py:459
  46.1 13.6 %collective-permute-start.10 = (f32[512,128]{1,0:T(8,128)S(1)}, f32[512,128]{1,0:T(8,128)S(1)}, u32[]{:S(2)}, u32[]{:S(2)}) collective-permute-start(f32[512,128]{1,0:T(8,128)S(1)} %get-tuple-element.58), channel_id=1, source_target_pairs={{0,32},{32,64},{64,96},{96,128},{128,160},{160,192},{192,224},{224... | collective-permute-start | bytes 786440 | tf_op jit(solution)/shard_map/ppermute | solution.py:459
  46.2 13.6 %collective-permute-start.11 = (f32[512,128]{1,0:T(8,128)S(1)}, f32[512,128]{1,0:T(8,128)S(1)}, u32[]{:S(2)}, u32[]{:S(2)}) collective-permute-start(f32[512,128]{1,0:T(8,128)S(1)} %get-tuple-element.59.loca), channel_id=1, source_target_pairs={{0,224},{32,0},{64,32},{96,64},{128,96},{160,128},{192,160},{224,1... | collective-permute-start | bytes 786440 | tf_op jit(solution)/shard_map/ppermute | solution.py:459
  48.9 6.3 %collective-permute-start.12 = (f32[2,128]{1,0:T(2,128)S(1)}, f32[2,128]{1,0:T(2,128)S(1)}, u32[]{:S(2)}, u32[]{:S(2)}) collective-permute-start(f32[2,128]{1,0:T(2,128)S(1)} %get-tuple-element.61), channel_id=1, source_target_pairs={{0,4},{4,8},{8,12},{12,16},{16,20},{20,24},{24,28},{28,0},{1,5},{5... | collective-permute-start | bytes 3080 | tf_op jit(solution)/shard_map/ppermute | solution.py:459
  53.9 5.9 %collective-permute-start.13 = (f32[2,128]{1,0:T(2,128)S(1)}, f32[2,128]{1,0:T(2,128)S(1)}, u32[]{:S(2)}, u32[]{:S(2)}) collective-permute-start(f32[2,128]{1,0:T(2,128)S(1)} %get-tuple-element.62), channel_id=1, source_target_pairs={{0,28},{4,0},{8,4},{12,8},{16,12},{20,16},{24,20},{28,24},{1,29},{... | collective-permute-start | bytes 3080 | tf_op jit(solution)/shard_map/ppermute | solution.py:459
  53.9 5.9 %collective-permute-start.14 = (f32[2,1024]{1,0:T(2,128)S(1)}, f32[2,1024]{1,0:T(2,128)S(1)}, u32[]{:S(2)}, u32[]{:S(2)}) collective-permute-start(f32[2,1024]{1,0:T(2,128)S(1)} %get-tuple-element.63), channel_id=1, source_target_pairs={{0,1},{1,2},{2,3},{3,0},{4,5},{5,6},{6,7},{7,4},{8,9},{9,10},{10,1... | collective-permute-start | bytes 24584 | tf_op jit(solution)/shard_map/ppermute | solution.py:459
  55.2 4.6 %collective-permute-start.15 = (f32[2,1024]{1,0:T(2,128)S(1)}, f32[2,1024]{1,0:T(2,128)S(1)}, u32[]{:S(2)}, u32[]{:S(2)}) collective-permute-start(f32[2,1024]{1,0:T(2,128)S(1)} %get-tuple-element.64), channel_id=1, source_target_pairs={{0,3},{1,0},{2,1},{3,2},{4,7},{5,4},{6,5},{7,6},{8,11},{9,8},{10,9... | collective-permute-start | bytes 24584 | tf_op jit(solution)/shard_map/ppermute | solution.py:459
